TPU v7x, 32 devices: a whole 2x2x4 slice. The times are simulated.
32 devices in a mesh: tm: 2 (over x), lon: 4 (over y, core), lat: 4 (over z).
Axes of the slice: x: 2, y: 2, z: 4, core: 2. Of those that a mesh axis runs over, the one named last changes fastest.
Arguments:
- iterate: float32 [2, 64, 64, 512], P('tm', None, 'lat', 'lon'), may hold values from -6 to 6
- heating: float32 [2, 64, 64, 512], P('tm', None, 'lat', 'lon'), may hold values from -6 to 6
- initial: float32 [64, 64, 512], P(None, 'lat', 'lon'), may hold values from -6 to 6
- region: int32 [64, 64, 512], P(None, 'lat', 'lon'), may hold values from 0 to 7
- cond_table: float32 [8], replicated, may hold values from 0.3 to 3
Outputs:
- updated: float32 [2, 64, 64, 512], P('tm', None, 'lat', 'lon')
Inputs may be any that keep to these rules, and one draw needn't show every extreme that they name: `region`: class index of each cell.
All inputs are finite; a program needn't handle non-finite values.
Results may differ from a plain program's by a relative error of at most 0.0003.
Values sent between devices are 32-bit elements; how exact they have to be, the bound alone decides.
No kernel may reach another device: no remote copies, remote signals or barrier semaphores. Data moves between devices by JAX's collectives and lax.ppermute only.
A program may use at most 128 MiB of HBM per device.

v0:
```python
import functools

import jax
import jax.numpy as jnp
from jax import lax
from jax.experimental import pallas as pl
from jax.experimental.pallas import tpu as pltpu
from jax.sharding import PartitionSpec as P

SWEEPS = 4


corner_weight = 0.1


def padded(value, sides, width, wrap):
    for axis, dim in sides:
        peers, length = (lax.axis_size(axis), value.shape[dim])
        up = [(i, (i + 1) % peers) for i in range(peers if wrap else peers - 1)]
        down = [(j, i) for i, j in up]
        last = lax.slice_in_dim(value, length - width, length, axis=dim)
        initial = lax.slice_in_dim(value, 0, width, axis=dim)
        before = lax.ppermute(last, axis, up)
        after = lax.ppermute(initial, axis, down)
        value = jnp.concatenate([before, value, after], axis=dim)
    return value


def passed_along(block, axis, distance):
    devices = range(lax.axis_size(axis))
    route = [(i - distance, i) for i in devices if i - distance in devices]
    return lax.ppermute(block, axis, route)


def harmonic(first, second):
    return 2.0 * first * second / (first + second)


def conductivity(region, cond_table):
    classes = jnp.arange(cond_table.shape[0], dtype=jnp.int32)
    onehot = (region[..., None] == classes).astype(jnp.float32)
    return jnp.sum(onehot * cond_table, axis=-1)


def extend(stack):
    lat_ext = padded(stack, (("lat", 2),), 1, False)
    both = padded(lat_ext, (("lon", 3),), 1, True)
    return jnp.pad(both, ((0, 0), (1, 1), (0, 0), (0, 0)))


def face_weights(kext):
    centre = kext[1:-1, 1:-1, 1:-1]
    return (
        harmonic(centre, kext[:-2, 1:-1, 1:-1]),
        harmonic(centre, kext[2:, 1:-1, 1:-1]),
        harmonic(centre, kext[1:-1, :-2, 1:-1]),
        harmonic(centre, kext[1:-1, 2:, 1:-1]),
        harmonic(centre, kext[1:-1, 1:-1, :-2]),
        harmonic(centre, kext[1:-1, 1:-1, 2:]),
    )


def neighbours(weights, ext):
    near = weights[0] * ext[..., :-2, 1:-1, 1:-1] + weights[1] * ext[..., 2:, 1:-1, 1:-1]
    near = near + weights[2] * ext[..., 1:-1, :-2, 1:-1] + weights[3] * ext[..., 1:-1, 2:, 1:-1]
    near = near + weights[4] * ext[..., 1:-1, 1:-1, :-2] + weights[5] * ext[..., 1:-1, 1:-1, 2:]
    return near


def on_device(iterate, heating, initial, region, cond_table):
    steps = lax.axis_size("tm")
    own = lax.axis_index("tm")
    high = lax.Precision.HIGHEST
    kfield = conductivity(region, cond_table)
    ext = extend(jnp.stack([kfield, iterate[0]]))
    weights = face_weights(ext[0])
    total = weights[0] + weights[1] + weights[2] + weights[3] + weights[4] + weights[5]
    shifted = passed_along(iterate, "tm", 1)[0]
    previous = jnp.where(own == 0, initial, shifted)
    residual = heating[0] + previous - ((1.0 + total) * iterate[0] - neighbours(weights, ext[1]))
    scale_own = corner_weight ** (own.astype(jnp.float32) / steps)
    scaled = residual * scale_own
    zeros = jnp.zeros_like(residual)
    piece = lax.all_gather(scaled[None], "tm", axis=0, tiled=True)
    order = jnp.arange(piece.shape[0], dtype=jnp.int32)
    angle = 2.0 * jnp.pi / steps * (own * order % steps).astype(jnp.float32)
    real_part = jnp.einsum("n,nabc->abc", jnp.cos(angle), piece, precision=high)
    imag_part = (zeros, zeros)[1] - jnp.einsum("n,nabc->abc", jnp.sin(angle), piece, precision=high)
    beta = corner_weight ** (1.0 / steps)
    freq_angle = 2.0 * jnp.pi / steps * (own % steps).astype(jnp.float32)
    diag_re = 1.0 - beta * jnp.cos(freq_angle) + total
    diag_im = beta * jnp.sin(freq_angle) + zeros
    denom = diag_re * diag_re + diag_im * diag_im
    inv_re = diag_re / denom
    inv_im = -diag_im / denom
    sol_re = real_part * inv_re - imag_part * inv_im
    sol_im = real_part * inv_im + imag_part * inv_re
    for sweep in range(SWEEPS - 1):
        near = neighbours(weights, extend(jnp.stack([sol_re, sol_im])))
        rhs_re = real_part + near[0]
        rhs_im = imag_part + near[1]
        sol_re = rhs_re * inv_re - rhs_im * inv_im
        sol_im = rhs_re * inv_im + rhs_im * inv_re
    pieces = (
        lax.all_gather(sol_re[None], "tm", axis=0, tiled=True),
        lax.all_gather(sol_im[None], "tm", axis=0, tiled=True),
    )
    order = jnp.arange(pieces[0].shape[0], dtype=jnp.int32)
    angle = 2.0 * jnp.pi / steps * (order * own % steps).astype(jnp.float32)
    summed = jnp.einsum("k,kabc->abc", jnp.cos(angle), pieces[0], precision=high) - jnp.einsum(
        "k,kabc->abc", jnp.sin(angle), pieces[1], precision=high
    )
    back = summed / steps
    return iterate + (back / scale_own)[None]


HALO = 4
TILE = 8
LEVELS = 64
ROWS = 16
LONS = 128
HALF = 64
SENT = HALF + HALO
PLACES = HALF + 2 * HALO
PAIRS = PLACES // 2
SENT_PAIRS = SENT // 2
QUADS = PLACES // 4
SPLIT = 26
FIXED = SPLIT
PARTNER = SPLIT + QUADS
CHUNKS = 4


def specs(count, hbm):
    return [pl.BlockSpec(memory_space=pltpu.HBM if i in hbm else pltpu.VMEM) for i in range(count)]


def call(body, outs, ins, scratch=(), limit=8, hbm_ins=(), hbm_outs=()):
    moved = sum(x.size * 4 for x in ins) + sum(x.size * 4 for x in outs)
    return pl.pallas_call(
        body,
        out_shape=outs,
        in_specs=specs(len(ins), hbm_ins),
        out_specs=specs(len(outs), hbm_outs),
        scratch_shapes=scratch,
        compiler_params=pltpu.CompilerParams(vmem_limit_bytes=limit << 20),
        cost_estimate=pl.CostEstimate(flops=moved * 4, bytes_accessed=moved, transcendentals=0),
    )(*ins)


def shape(*dims):
    return jax.ShapeDtypeStruct(dims, jnp.float32)


def buffer(*dims):
    return pltpu.VMEM(dims, jnp.float32)


def ids(rows, dim):
    return lax.broadcasted_iota(jnp.int32, (rows, 128), dim)


def in_low(rows):
    return ids(rows, 1) < LEVELS


def swapped(x):
    return pltpu.roll(x, LEVELS, 1)


def main_at(i):
    return jnp.where(lax.axis_index("tm") == 0, SENT - 1 - i, i)


def outer_at(i):
    return jnp.where(lax.axis_index("tm") == 0, PLACES - 1 - i, SENT + i)


def cat(*values):
    return jnp.concatenate(values, axis=0)


def even(axis):
    return lax.rem(lax.axis_index(axis), 2) == 0


def blocks(lo, hi, width, step):
    def body(i, carry):
        for u in range(width):
            step(lo + i * width + u)
        return carry

    lax.fori_loop(0, (hi - lo) // width, body, 0)


def send_first(it_hbm, h_hbm, edges, middle, turned, it, h, sems):
    t = lax.axis_index("tm")
    by_level = (LEVELS, ROWS, LONS)
    copies = []
    for k in range(ROWS // TILE):
        for f, (source, target) in enumerate(((it_hbm, it), (h_hbm, h))):
            for c in range(2):
                part = pl.ds(c * LEVELS // 2, LEVELS // 2), pl.ds(k * TILE, TILE)
                copy = pltpu.make_async_copy(source.at[part], target.reshape(by_level).at[part], sems.at[k, f, c])
                copy.start()
                copies.append(copy)

    def turn(r):
        rows = pl.ds(r, LEVELS, stride=ROWS)
        turned[pl.ds(r, LONS, stride=ROWS), :] = cat(it[rows, :], h[rows, :]).T

    for k in range(ROWS // TILE):
        for copy in copies[4 * k : 4 * k + 4]:
            copy.wait()
        blocks(k * TILE, (k + 1) * TILE, 4, turn)
    start = (LONS - SENT) * ROWS * (1 - t)
    top = ids(TILE, 0) < HALO

    def cut(i):
        at = pl.multiple_of(start + i * ROWS, ROWS)
        low, high = turned[pl.ds(at, TILE), :], turned[pl.ds(at + TILE, TILE), :]
        edges[i] = jnp.where(top, low, high)
        middle[i] = jnp.where(top, high, low)

    blocks(0, SENT, 17, cut)


def heated(turned, fixed):
    add = jnp.logical_and(jnp.logical_not(in_low(ROWS)), lax.axis_index("tm") == 0)
    return turned + jnp.where(add, fixed, 0.0)


def send_sides(turned, region, initial, table_hbm, fixed, near_sides, far_sides, table, sem):
    copy = pltpu.make_async_copy(table_hbm, table, sem)
    copy.start()
    copy.wait()

    def turn(r):
        rows = pl.ds(r, LEVELS, stride=ROWS)
        classes = region[rows, :]
        value = jnp.full(classes.shape, table[0], jnp.float32)
        for c in range(1, table.shape[0]):
            value = jnp.where(classes == c, table[c], value)
        fixed[pl.ds(r, LONS, stride=ROWS), :] = cat(value, initial[rows, :]).T

    blocks(0, ROWS, 4, turn)
    near_right = even("lon")
    low = in_low(ROWS)

    def strip(first_lon):
        def at(ref, i):
            return ref[(first_lon + i) * ROWS : (first_lon + i + 1) * ROWS, :]

        return [heated(at(turned, i), at(fixed, i)) for i in range(HALO)] + [
            jnp.where(low, at(fixed, i), swapped(at(fixed, i + 2))) for i in range(2)
        ]

    for i, (right, left) in enumerate(zip(strip(LONS - HALO), strip(0))):
        near_sides[i] = jnp.where(near_right, right, left)
        far_sides[i] = jnp.where(near_right, left, right)


def edge_pair(first, second):
    top = ids(TILE, 0) < HALO
    first_up = even("lat")
    down = jnp.where(top, first[:TILE], pltpu.roll(second[:TILE], HALO, 0))
    up = jnp.where(top, pltpu.roll(first[-TILE:], HALO, 0), second[-TILE:])
    return jnp.where(first_up, up, down), jnp.where(first_up, down, up)


def halo_tiles(near_pair, far_pair):
    first_up = even("lat")
    after = jnp.where(first_up, near_pair, far_pair)
    before = jnp.where(first_up, far_pair, near_pair)
    top = ids(TILE, 0) < HALO
    return (
        jnp.where(top, after, pltpu.roll(before, HALO, 0)),
        jnp.where(top, pltpu.roll(after, HALO, 0), before),
    )


def add_sides(turned, fixed, near_sides, far_sides, own, own_fixed, near_lat, far_lat, partner):
    t = lax.axis_index("tm")
    from_near = (t == 0) != even("lon")
    count = near_sides.shape[0]
    beside = [jnp.where(from_near, near_sides[i], far_sides[i]) for i in range(count)]
    other = [jnp.where(from_near, far_sides[i], near_sides[i]) for i in range(HALO)]
    for i in range(HALO):
        own[outer_at(i)] = beside[i]
        partner[i] = other[i]
    for i in range(2):
        own_fixed[outer_at(i)] = beside[HALO + i]
        own_fixed[outer_at(i + 2)] = swapped(beside[HALO + i])
        near_lat[PARTNER + i], far_lat[PARTNER + i] = edge_pair(other[i], other[i + 2])

    def copy(i):
        at = main_at(i)
        lon = (LONS - SENT) * t + i
        own[at] = heated(turned[lon], fixed[lon])
        own_fixed[at] = fixed[lon]

    blocks(0, SENT, 17, copy)

    def rows(i):
        near_lat[i], far_lat[i] = edge_pair(own[i], own[i + PAIRS])

    blocks(0, SPLIT, 13, rows)
    low = in_low(TILE)

    def fixed_rows(i):
        here = edge_pair(own_fixed[i], own_fixed[i + PAIRS])
        there = edge_pair(own_fixed[i + QUADS], own_fixed[i + PAIRS + QUADS])
        near_lat[FIXED + i], far_lat[FIXED + i] = [jnp.where(low, a, swapped(b)) for a, b in zip(here, there)]

    blocks(0, QUADS, 9, fixed_rows)


def start_of_step(fixed, rows):
    add = jnp.logical_and(jnp.logical_not(in_low(rows)), lax.axis_index("tm") == 1)
    return jnp.where(add, fixed, 0.0)


def pass_rows(edges, own, own_fixed, heated_edges, near_rows, far_rows):
    top = ids(TILE, 0) < HALO

    def heat(i):
        fixed = own_fixed[main_at(i)]
        heated_edges[i] = edges[i] + start_of_step(jnp.where(top, fixed[:TILE], fixed[TILE:]), TILE)

    blocks(0, SENT, 17, heat)

    def rows(i):
        near_rows[i], far_rows[i] = edge_pair(heated_edges[i], heated_edges[i + SENT_PAIRS])

    blocks(0, SENT_PAIRS, 17, rows)

    def rest(i):
        near_rows[SENT_PAIRS + i], far_rows[SENT_PAIRS + i] = edge_pair(own[SPLIT + i], own[SPLIT + i + PAIRS])

    blocks(0, PAIRS - SPLIT, 10, rest)


def join(near_lat, far_lat, near_rows, far_rows, halo, other):
    def place(i, tiles):
        halo[i], halo[i + PAIRS] = tiles

    blocks(0, SPLIT, 13, lambda i: place(i, halo_tiles(near_lat[i], far_lat[i])))

    def rest(i):
        at = SENT_PAIRS + i
        place(SPLIT + i, halo_tiles(near_rows[at], far_rows[at]))

    blocks(0, PAIRS - SPLIT, 10, rest)

    def theirs(i):
        other[main_at(i)], other[main_at(i + SENT_PAIRS)] = halo_tiles(near_rows[i], far_rows[i])

    blocks(0, SENT_PAIRS, 17, theirs)


def both_steps(mine, theirs):
    first = lax.axis_index("tm") == 0
    low = in_low(mine.shape[0])
    step0, step1 = jnp.where(first, mine, theirs), jnp.where(first, theirs, mine)
    moved = swapped(step0)
    return jnp.where(low, step0, swapped(step1)), jnp.where(low, moved, step1 + moved)


def gather(edges, middle, own, own_fixed, it, source):
    top = ids(TILE, 0) < HALO

    def step(i):
        at = main_at(i)
        fixed = own_fixed[at]
        e = edges[i]
        m = middle[i] + start_of_step(jnp.where(top, fixed[TILE:], fixed[:TILE]), TILE)
        theirs = cat(jnp.where(top, e, m), jnp.where(top, m, e))
        it[at], source[at] = both_steps(own[at], theirs)

    blocks(0, SENT, 17, step)


def strips(partner, near_lat, far_lat, xs):
    for i in range(2):
        at = PARTNER + i
        for place, tile in zip((i, i + 2), halo_tiles(near_lat[at], far_lat[at])):
            xs[place] = cat(partner[place], tile)


def reciprocal(d):
    y = pl.reciprocal(d, approx=True)
    return y * (2.0 - d * y)


def face(a, b):
    return 2.0 * a * b * reciprocal(jnp.maximum(a + b, 1e-30))


def woven(ref, at):
    return cat(*[ref[at, pl.ds(j, TILE, stride=3), :] for j in range(3)])


def next_row(x):
    return cat(x[TILE:], pltpu.roll(x[:TILE], TILE - 1, 0))


def last_row(x):
    return cat(pltpu.roll(x[-TILE:], 1, 0), x[:-TILE])


def near(around, w):
    before, mid, after = around
    wxp, wx, wy, wyp, wl = w
    total = wxp * before + wx * after
    total = total + (wy * next_row(mid) + wyp * last_row(mid))
    return total + (wl * pltpu.roll(mid, 127, 1) + pltpu.roll(wl * mid, 1, 1))


def prepare(own_fixed, near_lat, far_lat, _, wx, wy, wyp, wl, total, inv, K):
    rows = ROWS + TILE
    low = in_low(ROWS)
    low_tile = in_low(TILE)
    beta = corner_weight ** 0.5
    K[PLACES] = jnp.zeros((rows, 128), jnp.float32)

    def assemble_fixed(i):
        for at, tile in zip((i, i + PAIRS), halo_tiles(near_lat[FIXED + i], far_lat[FIXED + i])):
            moved = swapped(tile)
            for here, value in ((at, jnp.where(low_tile, tile, moved)), (at + QUADS, jnp.where(low_tile, moved, tile))):
                main = own_fixed[here]
                K[here] = cat(jnp.where(low, main, swapped(main)), value)

    blocks(0, QUADS, 9, assemble_fixed)
    lane = ids(rows, 1)
    inside = (lane & (LEVELS - 1)) != LEVELS - 1
    shift = jnp.where(lane < LEVELS, 1.0 - beta, 1.0 + beta)
    width = 18

    def weigh(i, carry):
        start = i * width
        here = woven(K, start)
        before = wx[jnp.maximum(start - 1, 0)]
        for u in range(width):
            at = start + u
            after = woven(K, at + 1)
            side = face(here, after)
            row = face(here, next_row(here))
            previous = last_row(row)
            level = jnp.where(inside, face(here, pltpu.roll(here, 127, 1)), 0.0)
            sums = (before + side) + (row + previous) + (level + pltpu.roll(level, 1, 1))
            wx[at], wy[at], wyp[at], wl[at] = side, row, previous, level
            total[at] = sums
            inv[at] = reciprocal(shift + sums)
            here, before = after, side
        return carry

    wx[0] = jnp.zeros((rows, 128), jnp.float32)
    lax.fori_loop(0, PLACES // width, weigh, 0)


STAGES = ((1, 39, 71), (2, 38, 70), (3, 37, 69), (4, 36, 68))
WIDTHS = ((19, 12, 17, 16), (16, 16, 16, 16))
READY = 40
EDGE = 12


def iterate_half(
    upper, wx, wy, wyp, wl, total, inv, own, own_halo, other_halo, it_main, source_main, *refs
):
    if upper:
        xs, edge, w_own, w_send, *refs = refs
    else:
        w_own, w_send, edge, *refs = refs
    it, source, spec, x, y, z, natural = refs
    rows = ROWS + TILE
    first = lax.axis_index("tm") == 0
    low = in_low(rows)
    beta = corner_weight ** 0.5
    gamma = jnp.where(low, 1.0, beta)
    shared = [(it, 38), (it, 39), (source, 39), (x, 37), (x, 38), (y, 36), (y, 37), (z, 35), (z, 36)]
    shared += [(spec, 36), (spec, 37), (spec, 38)]
    if upper:
        for i, (ref, at) in enumerate(shared):
            ref[at] = edge[i]

    def assemble(at):
        a, b = both_steps(own_halo[at], other_halo[at])
        it[at], source[at] = cat(it_main[at], a), cat(source_main[at], b)

    if upper:
        blocks(READY, SENT, 14, assemble)
        for i in range(HALO):
            at = outer_at(i)
            it[at], source[at] = both_steps(cat(own[at], own_halo[at]), xs[i])
    else:
        blocks(0, READY, 10, assemble)

    def over(stage, read, ref, step):
        lo, hi = STAGES[stage][upper : upper + 2]
        width = WIDTHS[upper][stage]

        def body(i, carry):
            start = lo + i * width
            around = [read(ref, start - 1), read(ref, start)]
            before = wx[start - 1]
            for u in range(width):
                at = start + u
                around = [*around[-2:], read(ref, at + 1)]
                side = wx[at]
                step(at, around, (before, side, wy[at], wyp[at], wl[at]))
                before = side
            return carry

        lax.fori_loop(0, (hi - lo) // width, body, 0)

    def residual(at, around, w):
        left = (woven(source, at) - ((1.0 + total[at]) * around[1] - near(around, w))) * gamma
        moved = swapped(left)
        value = jnp.where(low, left + moved, moved - left)
        spec[at] = value
        x[at] = value * inv[at]

    over(0, woven, it, residual)

    def plain(ref, at):
        return ref[at]

    def sweep(at, around, w):
        return (spec[at] + near(around, w)) * inv[at]

    def to(ref):
        def step(at, around, w):
            ref[at] = sweep(at, around, w)

        return step

    over(1, plain, x, to(y))
    over(2, plain, y, to(z))
    base = STAGES[3][upper]
    back = jnp.where(low, 0.5, 0.5 / beta)

    def last(at, around, w):
        value = sweep(at, around, w)
        moved = swapped(value)
        value = jnp.where(low, value + moved, moved - value) * back
        lon = at - base
        lon = jnp.where(first, HALF // 2 - 1 - lon, lon)
        for j in range(3):
            natural[pl.ds(lon * rows + j, TILE, stride=3), :] = value[j * TILE : (j + 1) * TILE]

    over(3, plain, z, last)
    count = HALF // 2
    for q in range(4):
        turned = cat(*[natural[pl.ds(q + 4 * j, count, stride=rows), :] for j in range(4)]).T
        step0, step1 = turned[:LEVELS], turned[LEVELS:]
        w_own[q] = jnp.where(first, step0, step1)
        w_send[q] = jnp.where(first, step1, step0)
    if not upper:
        for i, (ref, at) in enumerate(shared):
            edge[i] = ref[at]


def placed(value, j, quarter):
    return pltpu.roll(value, (32 * (quarter - j) + 128) & 127, 1)


def finish_most(it, own_low, own_high, got_low, most):
    t = lax.axis_index("tm")
    group = ids(LEVELS, 1) // 32

    def step(q):
        for j in range(4):
            rows = pl.ds(q + 4 * j, LEVELS, stride=ROWS)
            value = it[rows, :]
            for piece, quarter in ((own_low, 1 + t), (own_high, 3 * t), (got_low, 2 - t)):
                value = jnp.where(group == quarter, value + placed(piece[q], j, quarter), value)
            most[rows, :] = value

    blocks(0, 4, 2, step)


def finish(most, got_high, out_hbm, out, sems):
    quarter = 3 - 3 * lax.axis_index("tm")
    part = LEVELS // CHUNKS
    here = ids(part, 1) // 32 == quarter

    def copy(c):
        span = pl.ds(pl.multiple_of(c * part * ROWS, part * ROWS), part * ROWS)
        return pltpu.make_async_copy(out.at[span], out_hbm.at[span], sems.at[c])

    def step(c):
        for q in range(4):
            value = got_high[q, pl.ds(pl.multiple_of(c * part, part), part), :]
            for j in range(4):
                rows = pl.ds(c * part * ROWS + q + 4 * j, part, stride=ROWS)
                old = most[rows, :]
                out[rows, :] = jnp.where(here, old + placed(value, j, quarter), old)
        copy(c).start()

    blocks(0, CHUNKS, 1, step)
    for c in range(CHUNKS):
        copy(c).wait()


def two_steps(iterate, heating, initial, region, cond_table):
    lats, lons = lax.axis_size("lat"), lax.axis_size("lon")
    swap = [(0, 1), (1, 0)]
    pairs = [[(i, i + 1) for i in range(start, lats - 1, 2)] for start in (0, 1)]
    pairs = [p + [(j, i) for i, j in p] for p in pairs]
    round_lon = [[(i, (i + 1) % lons) for i in range(start, lons, 2)] for start in (0, 1)]
    round_lon = [p + [(j, i) for i, j in p] for p in round_lon]
    flat = (LEVELS * ROWS, LONS)
    turned_flat = (LONS * ROWS, 2 * LEVELS)
    by_lon = (LONS, ROWS, 2 * LEVELS)
    wide = shape(PLACES, ROWS + TILE, 128)

    def in_hbm(x):
        return pltpu.with_memory_space_constraint(x, pltpu.HBM)

    half_rows = shape(SENT, TILE, 128)
    edges, middle, turned, it = call(
        send_first,
        [half_rows, half_rows, shape(*turned_flat), shape(*flat)],
        [in_hbm(iterate[0]), in_hbm(heating[0])],
        scratch=[buffer(*flat), pltpu.SemaphoreType.DMA((ROWS // TILE, 2, 2))],
        hbm_ins=(0, 1),
    )
    edges = lax.ppermute(edges, "tm", swap)
    middle = lax.ppermute(middle, "tm", swap)
    sides = shape(HALO + 2, ROWS, 128)
    fixed, near_sides, far_sides = call(
        send_sides,
        [shape(*turned_flat), sides, sides],
        [turned, region.reshape(flat), initial.reshape(flat), in_hbm(cond_table)],
        scratch=[pltpu.SMEM(cond_table.shape, jnp.float32), pltpu.SemaphoreType.DMA],
        hbm_ins=(3,),
    )
    near_sides = lax.ppermute(near_sides, "lon", round_lon[0])
    far_sides = lax.ppermute(far_sides, "lon", round_lon[1])
    main = shape(PLACES, ROWS, 128)
    lat = shape(PARTNER + 2, TILE, 128)
    own_main, own_fixed, near_lat, far_lat, partner = call(
        add_sides,
        [main, main, lat, lat, shape(HALO, ROWS, 128)],
        [turned.reshape(by_lon), fixed.reshape(by_lon), near_sides, far_sides],
    )
    near_lat = lax.ppermute(near_lat, "lat", pairs[0])
    far_lat = lax.ppermute(far_lat, "lat", pairs[1])
    rows = shape(SENT_PAIRS + PAIRS - SPLIT, TILE, 128)
    edges, near_rows, far_rows = call(pass_rows, [half_rows, rows, rows], [edges, own_main, own_fixed])
    near_rows = lax.ppermute(near_rows, "lat", pairs[0])
    far_rows = lax.ppermute(far_rows, "lat", pairs[1])
    it_main, source_main = call(gather, [main, main], [edges, middle, own_main, own_fixed])
    (xs,) = call(strips, [shape(HALO, ROWS + TILE, 128)], [partner, near_lat, far_lat])
    xs = lax.ppermute(xs, "tm", swap)
    ready = call(
        prepare,
        [wide] * 6,
        [own_fixed, near_lat, far_lat, it_main],
        scratch=[buffer(PLACES + 1, ROWS + TILE, 128)],
    )
    halos = call(join, [shape(PLACES, TILE, 128)] * 2, [near_lat, far_lat, near_rows, far_rows])
    given = [*ready, own_main, *halos, it_main, source_main]
    corrections = [shape(4, LEVELS, 128)] * 2
    fields = [buffer(PLACES, ROWS + TILE, 128)] * 6 + [buffer(HALF // 2 * (ROWS + TILE), 128)]
    own_low, send_low, edge = call(
        functools.partial(iterate_half, 0),
        [*corrections, shape(EDGE, ROWS + TILE, 128)],
        given,
        scratch=fields,
        limit=16,
    )
    got_low = lax.ppermute(send_low, "tm", swap)
    own_high, send_high = call(
        functools.partial(iterate_half, 1), corrections, [*given, xs, edge], scratch=fields, limit=16
    )
    got_high = lax.ppermute(send_high, "tm", swap)
    (most,) = call(finish_most, [shape(*flat)], [it, own_low, own_high, got_low])
    (out,) = call(
        finish,
        [shape(*flat)],
        [most, got_high],
        scratch=[buffer(*flat), pltpu.SemaphoreType.DMA((CHUNKS,))],
        hbm_outs=(0,),
    )
    return out.reshape(iterate.shape)


def solution(mesh):
    return jax.shard_map(
        two_steps if mesh.shape["tm"] == 2 else on_device,
        mesh=mesh,
        in_specs=(
            P("tm", None, "lat", "lon"),
            P("tm", None, "lat", "lon"),
            P(None, "lat", "lon"),
            P(None, "lat", "lon"),
            P(),
        ),
        out_specs=P("tm", None, "lat", "lon"),
        check_vma=False,
    )
```

profile of v0, /device:TPU:16, one launch (start us, length us, event | category | flops | bytes accessed | tf_op | source)
XLA Modules:
  0.0 36.4 jit_solution(9482620980999471840)
XLA Ops:
  0.0 1.9 %shard_map.55 = (f32[68,8,128]{2,1,0:T(8,128)S(1)}, f32[68,8,128]{2,1,0:T(8,128)S(1)}, f32[2048,128]{1,0:T(8,128)S(1)}, f32[1024,128]{1,0:T(8,128)S(1)}) custom-call(f32[64,16,128]{2,1,0:T(8,128)} %bitcast.11, f32[64,16,128]{2,1,0:T(8,128)} %bitcast.12), custom_call_target="tpu_custom_call" | custom-call | flops 12713984 | bytes 3178496 | tf_op jit(solution)/shard_map/pallas_call | solution.py:140
  1.9 1.6 %collective-permute-start.4 = (f32[68,8,128]{2,1,0:T(8,128)S(1)}, f32[68,8,128]{2,1,0:T(8,128)S(1)}, u32[]{:S(2)}, u32[]{:S(2)}) collective-permute-start(f32[68,8,128]{2,1,0:T(8,128)S(1)} %get-tuple-element.43), channel_id=1, source_target_pairs={{0,16},{16,0},{1,17},{17,1},{2,18},{18,2},{3,19},{19,3},{4,20},{20... | collective-permute-start | bytes 835592 | tf_op jit(solution)/shard_map/ppermute | solution.py:628
  3.5 1.5 %shard_map.56 = (f32[2048,128]{1,0:T(8,128)S(1)}, f32[6,16,128]{2,1,0:T(8,128)S(1)}, f32[6,16,128]{2,1,0:T(8,128)S(1)}) custom-call(f32[2048,128]{1,0:T(8,128)S(1)} %get-tuple-element.36.turned, s32[1024,128]{1,0:T(8,128)S(1)} %bitcast.9, f32[1024,128]{1,0:T(8,128)S(1)} %bitcast.10, f32[8]{0:T(128)} %table_hbm.1), custom_call_target="tpu_custom_call" | custom-call | flops 12976256 | bytes 3244064 | tf_op jit(solution)/shard_map/pallas_call | solution.py:140
  5.0 0.1 collective-permute-start
  5.1 1.6 %collective-permute-start.1 = (f32[6,16,128]{2,1,0:T(8,128)S(1)}, f32[6,16,128]{2,1,0:T(8,128)S(1)}, u32[]{:S(2)}, u32[]{:S(2)}) collective-permute-start(f32[6,16,128]{2,1,0:T(8,128)S(1)} %get-tuple-element.39), channel_id=1, source_target_pairs={{4,8},{12,0},{8,4},{0,12},{5,9},{13,1},{9,5},{1,13},{6,10},{14,2},... | collective-permute-start | bytes 147464 | tf_op jit(solution)/shard_map/ppermute | solution.py:639
  6.7 0.5 %collective-permute-start.5 = (f32[68,8,128]{2,1,0:T(8,128)S(1)}, f32[68,8,128]{2,1,0:T(8,128)S(1)}, u32[]{:S(2)}, u32[]{:S(2)}) collective-permute-start(f32[68,8,128]{2,1,0:T(8,128)S(1)} %get-tuple-element.46), channel_id=1, source_target_pairs={{0,16},{16,0},{1,17},{17,1},{2,18},{18,2},{3,19},{19,3},{4,20},{20... | collective-permute-start | bytes 835592 | tf_op jit(solution)/shard_map/ppermute | solution.py:629
  7.2 0.0 collective-permute-done.near_sides
  7.2 1.4 %collective-permute-done.1.far_sides = f32[6,16,128]{2,1,0:T(8,128)S(1)} collective-permute-done((f32[6,16,128]{2,1,0:T(8,128)S(1)}, f32[6,16,128]{2,1,0:T(8,128)S(1)}, u32[]{:S(2)}, u32[]{:S(2)}) %collective-permute-start.1) | collective-permute-done | bytes 49184 | tf_op jit(solution)/shard_map/ppermute | solution.py:639
  8.6 0.4 %shard_map.57 = (f32[72,16,128]{2,1,0:T(8,128)S(1)}, f32[72,16,128]{2,1,0:T(8,128)S(1)}, f32[46,8,128]{2,1,0:T(8,128)S(1)}, f32[46,8,128]{2,1,0:T(8,128)S(1)}, f32[4,16,128]{2,1,0:T(8,128)S(1)}) custom-call(f32[128,16,128]{2,1,0:T(8,128)S(1)} %bitcast.7, f32[128,16,128]{2,1,0:T(8,128)S(1)} %bitcast.8, f32[6,16,128]{2,1,0:T(8,128)S(1)} %collective-permute-done.near_sides, ...), custom_call_target="tpu_custom_call" | custom-call | flops 15138816 | bytes 3784704 | tf_op jit(solution)/shard_map/pallas_call | solution.py:140
  9.1 1.6 %collective-permute-start.2 = (f32[46,8,128]{2,1,0:T(8,128)S(1)}, f32[46,8,128]{2,1,0:T(8,128)S(1)}, u32[]{:S(2)}, u32[]{:S(2)}) collective-permute-start(f32[46,8,128]{2,1,0:T(8,128)S(1)} %get-tuple-element.41), channel_id=1, source_target_pairs={{0,1},{2,3},{1,0},{3,2},{4,5},{6,7},{5,4},{7,6},{8,9},{10,11},{9,8... | collective-permute-start | bytes 565256 | tf_op jit(solution)/shard_map/ppermute | solution.py:647
  10.7 1.9 %collective-permute-start.3 = (f32[46,8,128]{2,1,0:T(8,128)S(1)}, f32[46,8,128]{2,1,0:T(8,128)S(1)}, u32[]{:S(2)}, u32[]{:S(2)}) collective-permute-start(f32[46,8,128]{2,1,0:T(8,128)S(1)} %get-tuple-element.42), channel_id=1, source_target_pairs={{1,2},{2,1},{5,6},{6,5},{9,10},{10,9},{13,14},{14,13},{17,18},{18,... | collective-permute-start | bytes 565256 | tf_op jit(solution)/shard_map/ppermute | solution.py:648
  12.6 0.0 collective-permute-done.4.edges
  12.6 0.2 shard_map.58
  12.8 0.4 collective-permute-start.6
  13.2 3.6 %collective-permute-start.7 = (f32[44,8,128]{2,1,0:T(8,128)S(1)}, f32[44,8,128]{2,1,0:T(8,128)S(1)}, u32[]{:S(2)}, u32[]{:S(2)}) collective-permute-start(f32[44,8,128]{2,1,0:T(8,128)S(1)} %get-tuple-element.55), channel_id=1, source_target_pairs={{1,2},{2,1},{5,6},{6,5},{9,10},{10,9},{13,14},{14,13},{17,18},{18,... | collective-permute-start | bytes 540680 | tf_op jit(solution)/shard_map/ppermute | solution.py:652
  16.8 0.0 collective-permute-done.2.near_lat
  16.8 3.3 %collective-permute-done.3.far_lat = f32[46,8,128]{2,1,0:T(8,128)S(1)} collective-permute-done((f32[46,8,128]{2,1,0:T(8,128)S(1)}, f32[46,8,128]{2,1,0:T(8,128)S(1)}, u32[]{:S(2)}, u32[]{:S(2)}) %collective-permute-start.3) | collective-permute-done | bytes 188448 | tf_op jit(solution)/shard_map/ppermute | solution.py:648
  20.1 0.6 %collective-permute-start.8 = (f32[4,24,128]{2,1,0:T(8,128)S(1)}, f32[4,24,128]{2,1,0:T(8,128)S(1)}, u32[]{:S(2)}, u32[]{:S(2)}) collective-permute-start(f32[4,24,128]{2,1,0:T(8,128)S(1)} %shard_map.63), channel_id=1, source_target_pairs={{0,16},{16,0},{1,17},{17,1},{2,18},{18,2},{3,19},{19,3},{4,20},{20... | collective-permute-start | bytes 147464 | tf_op jit(solution)/shard_map/ppermute | solution.py:655
  20.7 0.0 collective-permute-done.5.middle
  20.7 0.6 %shard_map.59 = (f32[72,16,128]{2,1,0:T(8,128)S(1)}, f32[72,16,128]{2,1,0:T(8,128)S(1)}) custom-call(f32[68,8,128]{2,1,0:T(8,128)S(1)} %get-tuple-element.45.edges, f32[68,8,128]{2,1,0:T(8,128)S(1)} %collective-permute-done.5.middle, f32[72,16,128]{2,1,0:T(8,128)S(1)} %get-tuple-element.44.own, f32[72,16,128]{2,1,0:T(8,128)S(1)} %get-tuple-element.40.own_fixed), custom_call_target="tpu_custom_call" | custom-call | flops 11665408 | bytes 2916352 | tf_op jit(solution)/shard_map/pallas_call | solution.py:140
  21.3 1.6 %shard_map.60 = (f32[72,24,128]{2,1,0:T(8,128)S(1)}, f32[72,24,128]{2,1,0:T(8,128)S(1)}, f32[72,24,128]{2,1,0:T(8,128)S(1)}, f32[72,24,128]{2,1,0:T(8,128)S(1)},...) custom-call(f32[72,16,128]{2,1,0:T(8,128)S(1)} %get-tuple-element.40.own_fixed, ...), custom_call_target="tpu_custom_call" | custom-call | flops 27459584 | bytes 6864896 | tf_op jit(solution)/shard_map/pallas_call | solution.py:140
  22.9 0.0 collective-permute-done.6.near_rows
  22.9 0.6 %collective-permute-done.7.far_rows = f32[44,8,128]{2,1,0:T(8,128)S(1)} collective-permute-done((f32[44,8,128]{2,1,0:T(8,128)S(1)}, f32[44,8,128]{2,1,0:T(8,128)S(1)}, u32[]{:S(2)}, u32[]{:S(2)}) %collective-permute-start.7) | collective-permute-done | bytes 180256 | tf_op jit(solution)/shard_map/ppermute | solution.py:652
  23.5 0.2 shard_map.61
  23.7 3.1 %shard_map.62 = (f32[4,64,128]{2,1,0:T(8,128)S(1)}, f32[4,64,128]{2,1,0:T(8,128)S(1)}, f32[12,24,128]{2,1,0:T(8,128)S(1)}) custom-call(f32[72,24,128]{2,1,0:T(8,128)S(1)} %get-tuple-element.48.wx, f32[72,24,128]{2,1,0:T(8,128)S(1)} %get-tuple-element.49.wy, f32[72,24,128]{2,1,0:T(8,128)S(1)} %get-tuple-element.50.wyp, ...), custom_call_target="tpu_custom_call" | custom-call | flops 32309248 | bytes 8077312 | tf_op jit(solution)/shard_map/pallas_call | solution.py:140
  26.8 0.9 %collective-permute-start.9 = (f32[4,64,128]{2,1,0:T(8,128)S(1)}, f32[4,64,128]{2,1,0:T(8,128)S(1)}, u32[]{:S(2)}, u32[]{:S(2)}) collective-permute-start(f32[4,64,128]{2,1,0:T(8,128)S(1)} %get-tuple-element.63), channel_id=1, source_target_pairs={{0,16},{16,0},{1,17},{17,1},{2,18},{18,2},{3,19},{19,3},{4,20},{20... | collective-permute-start | bytes 393224 | tf_op jit(solution)/shard_map/ppermute | solution.py:673
  27.7 2.4 %shard_map.64 = (f32[4,64,128]{2,1,0:T(8,128)S(1)}, f32[4,64,128]{2,1,0:T(8,128)S(1)}) custom-call(f32[72,24,128]{2,1,0:T(8,128)S(1)} %get-tuple-element.48.wx, f32[72,24,128]{2,1,0:T(8,128)S(1)} %get-tuple-element.49.wy, f32[72,24,128]{2,1,0:T(8,128)S(1)} %get-tuple-element.50.wyp, f32[72,24,128]{2,1,0:T(8,128)S(1)} %get-tuple-element.51.wl, ...), custom_call_target="tpu_custom_call" | custom-call | flops 32505856 | bytes 8126464 | tf_op jit(solution)/shard_map/pallas_call | solution.py:140
  30.1 1.2 %collective-permute-start.10 = (f32[4,64,128]{2,1,0:T(8,128)S(1)}, f32[4,64,128]{2,1,0:T(8,128)S(1)}, u32[]{:S(2)}, u32[]{:S(2)}) collective-permute-start(f32[4,64,128]{2,1,0:T(8,128)S(1)} %get-tuple-element.64), channel_id=1, source_target_pairs={{0,16},{16,0},{1,17},{17,1},{2,18},{18,2},{3,19},{19,3},{4,20},{20... | collective-permute-start | bytes 393224 | tf_op jit(solution)/shard_map/ppermute | solution.py:677
  31.3 0.6 %collective-permute-done.9.got_low = f32[4,64,128]{2,1,0:T(8,128)S(1)} collective-permute-done((f32[4,64,128]{2,1,0:T(8,128)S(1)}, f32[4,64,128]{2,1,0:T(8,128)S(1)}, u32[]{:S(2)}, u32[]{:S(2)}) %collective-permute-start.9) | collective-permute-done | bytes 131104 | tf_op jit(solution)/shard_map/ppermute | solution.py:673
  31.9 0.7 %shard_map.65.most = f32[1024,128]{1,0:T(8,128)S(1)} custom-call(f32[1024,128]{1,0:T(8,128)S(1)} %get-tuple-element.35.it, f32[4,64,128]{2,1,0:T(8,128)S(1)} %get-tuple-element.59.own_low, f32[4,64,128]{2,1,0:T(8,128)S(1)} %get-tuple-element.62.own_high, f32[4,64,128]{2,1,0:T(8,128)S(1)} %collective-permute-done.9.got_low), custom_call_target="tpu_custom_call" | custom-call | flops 5767168 | bytes 1441792 | tf_op jit(solution)/shard_map/pallas_call | solution.py:140
  32.6 2.6 %collective-permute-done.10.got_high = f32[4,64,128]{2,1,0:T(8,128)S(1)} collective-permute-done((f32[4,64,128]{2,1,0:T(8,128)S(1)}, f32[4,64,128]{2,1,0:T(8,128)S(1)}, u32[]{:S(2)}, u32[]{:S(2)}) %collective-permute-start.10) | collective-permute-done | bytes 131104 | tf_op jit(solution)/shard_map/ppermute | solution.py:677
  35.2 1.2 %shard_map.66 = f32[1024,128]{1,0:T(8,128)} custom-call(f32[1024,128]{1,0:T(8,128)S(1)} %shard_map.65.most, f32[4,64,128]{2,1,0:T(8,128)S(1)} %collective-permute-done.10.got_high), custom_call_target="tpu_custom_call" | custom-call | flops 4718592 | bytes 1179648 | tf_op jit(solution)/shard_map/pallas_call | solution.py:140
  (6 shorter events, 0.0 us)
Async XLA Ops:
  0.0 3.5 %copy-start = (s32[64,16,128]{2,1,0:T(8,128)S(1)}, s32[64,16,128]{2,1,0:T(8,128)}, u32[]{:S(2)}) copy-start(s32[64,16,128]{2,1,0:T(8,128)} %param.8) | copy-start | bytes 1572868
  0.0 3.5 %copy-start.1 = (f32[64,16,128]{2,1,0:T(8,128)S(1)}, f32[64,16,128]{2,1,0:T(8,128)}, u32[]{:S(2)}) copy-start(f32[64,16,128]{2,1,0:T(8,128)} %param.7) | copy-start | bytes 1572868
  1.9 10.7 %collective-permute-start.4 = (f32[68,8,128]{2,1,0:T(8,128)S(1)}, f32[68,8,128]{2,1,0:T(8,128)S(1)}, u32[]{:S(2)}, u32[]{:S(2)}) collective-permute-start(f32[68,8,128]{2,1,0:T(8,128)S(1)} %get-tuple-element.43), channel_id=1, source_target_pairs={{0,16},{16,0},{1,17},{17,1},{2,18},{18,2},{3,19},{19,3},{4,20},{20... | collective-permute-start | bytes 835592 | tf_op jit(solution)/shard_map/ppermute | solution.py:628
  5.0 2.3 %collective-permute-start = (f32[6,16,128]{2,1,0:T(8,128)S(1)}, f32[6,16,128]{2,1,0:T(8,128)S(1)}, u32[]{:S(2)}, u32[]{:S(2)}) collective-permute-start(f32[6,16,128]{2,1,0:T(8,128)S(1)} %get-tuple-element.38), channel_id=1, source_target_pairs={{0,4},{8,12},{4,0},{12,8},{1,5},{9,13},{5,1},{13,9},{2,6},{10,14},... | collective-permute-start | bytes 147464 | tf_op jit(solution)/shard_map/ppermute | solution.py:638
  5.1 3.6 %collective-permute-start.1 = (f32[6,16,128]{2,1,0:T(8,128)S(1)}, f32[6,16,128]{2,1,0:T(8,128)S(1)}, u32[]{:S(2)}, u32[]{:S(2)}) collective-permute-start(f32[6,16,128]{2,1,0:T(8,128)S(1)} %get-tuple-element.39), channel_id=1, source_target_pairs={{4,8},{12,0},{8,4},{0,12},{5,9},{13,1},{9,5},{1,13},{6,10},{14,2},... | collective-permute-start | bytes 147464 | tf_op jit(solution)/shard_map/ppermute | solution.py:639
  6.7 14.0 %collective-permute-start.5 = (f32[68,8,128]{2,1,0:T(8,128)S(1)}, f32[68,8,128]{2,1,0:T(8,128)S(1)}, u32[]{:S(2)}, u32[]{:S(2)}) collective-permute-start(f32[68,8,128]{2,1,0:T(8,128)S(1)} %get-tuple-element.46), channel_id=1, source_target_pairs={{0,16},{16,0},{1,17},{17,1},{2,18},{18,2},{3,19},{19,3},{4,20},{20... | collective-permute-start | bytes 835592 | tf_op jit(solution)/shard_map/ppermute | solution.py:629
  9.1 7.8 %collective-permute-start.2 = (f32[46,8,128]{2,1,0:T(8,128)S(1)}, f32[46,8,128]{2,1,0:T(8,128)S(1)}, u32[]{:S(2)}, u32[]{:S(2)}) collective-permute-start(f32[46,8,128]{2,1,0:T(8,128)S(1)} %get-tuple-element.41), channel_id=1, source_target_pairs={{0,1},{2,3},{1,0},{3,2},{4,5},{6,7},{5,4},{7,6},{8,9},{10,11},{9,8... | collective-permute-start | bytes 565256 | tf_op jit(solution)/shard_map/ppermute | solution.py:647
  10.7 9.4 %collective-permute-start.3 = (f32[46,8,128]{2,1,0:T(8,128)S(1)}, f32[46,8,128]{2,1,0:T(8,128)S(1)}, u32[]{:S(2)}, u32[]{:S(2)}) collective-permute-start(f32[46,8,128]{2,1,0:T(8,128)S(1)} %get-tuple-element.42), channel_id=1, source_target_pairs={{1,2},{2,1},{5,6},{6,5},{9,10},{10,9},{13,14},{14,13},{17,18},{18,... | collective-permute-start | bytes 565256 | tf_op jit(solution)/shard_map/ppermute | solution.py:648
  12.8 10.1 %collective-permute-start.6 = (f32[44,8,128]{2,1,0:T(8,128)S(1)}, f32[44,8,128]{2,1,0:T(8,128)S(1)}, u32[]{:S(2)}, u32[]{:S(2)}) collective-permute-start(f32[44,8,128]{2,1,0:T(8,128)S(1)} %get-tuple-element.54), channel_id=1, source_target_pairs={{0,1},{2,3},{1,0},{3,2},{4,5},{6,7},{5,4},{7,6},{8,9},{10,11},{9,8... | collective-permute-start | bytes 540680 | tf_op jit(solution)/shard_map/ppermute | solution.py:651
  13.2 10.3 %collective-permute-start.7 = (f32[44,8,128]{2,1,0:T(8,128)S(1)}, f32[44,8,128]{2,1,0:T(8,128)S(1)}, u32[]{:S(2)}, u32[]{:S(2)}) collective-permute-start(f32[44,8,128]{2,1,0:T(8,128)S(1)} %get-tuple-element.55), channel_id=1, source_target_pairs={{1,2},{2,1},{5,6},{6,5},{9,10},{10,9},{13,14},{14,13},{17,18},{18,... | collective-permute-start | bytes 540680 | tf_op jit(solution)/shard_map/ppermute | solution.py:652
  20.1 7.6 %collective-permute-start.8 = (f32[4,24,128]{2,1,0:T(8,128)S(1)}, f32[4,24,128]{2,1,0:T(8,128)S(1)}, u32[]{:S(2)}, u32[]{:S(2)}) collective-permute-start(f32[4,24,128]{2,1,0:T(8,128)S(1)} %shard_map.63), channel_id=1, source_target_pairs={{0,16},{16,0},{1,17},{17,1},{2,18},{18,2},{3,19},{19,3},{4,20},{20... | collective-permute-start | bytes 147464 | tf_op jit(solution)/shard_map/ppermute | solution.py:655
  26.8 5.2 %collective-permute-start.9 = (f32[4,64,128]{2,1,0:T(8,128)S(1)}, f32[4,64,128]{2,1,0:T(8,128)S(1)}, u32[]{:S(2)}, u32[]{:S(2)}) collective-permute-start(f32[4,64,128]{2,1,0:T(8,128)S(1)} %get-tuple-element.63), channel_id=1, source_target_pairs={{0,16},{16,0},{1,17},{17,1},{2,18},{18,2},{3,19},{19,3},{4,20},{20... | collective-permute-start | bytes 393224 | tf_op jit(solution)/shard_map/ppermute | solution.py:673
  30.1 5.0 %collective-permute-start.10 = (f32[4,64,128]{2,1,0:T(8,128)S(1)}, f32[4,64,128]{2,1,0:T(8,128)S(1)}, u32[]{:S(2)}, u32[]{:S(2)}) collective-permute-start(f32[4,64,128]{2,1,0:T(8,128)S(1)} %get-tuple-element.64), channel_id=1, source_target_pairs={{0,16},{16,0},{1,17},{17,1},{2,18},{18,2},{3,19},{19,3},{4,20},{20... | collective-permute-start | bytes 393224 | tf_op jit(solution)/shard_map/ppermute | solution.py:677
where the time goes:
time: 36.5 us; the launch traced here: 36.4 us
  starting transfers between devices  14.1 us (39%)
  Pallas kernels  13.7 us (38%)
  waiting for transfers between devices  8.46 us (23%)
    pallas_call x12, Pallas kernels, call(): pl.pallas_call(body, out_shape=outs, in_specs=specs(len(ins), hbm_ins), o...  13.7 us
    ppermute x1, starting transfers between devices, two_steps(): far_rows = lax.ppermute(far_rows, 'lat', pairs[1])  3.64 us
    ppermute x1, waiting for transfers between devices, two_steps(): far_lat = lax.ppermute(far_lat, 'lat', pairs[1])  3.26 us
    ppermute x1, waiting for transfers between devices, two_steps(): got_high = lax.ppermute(send_high, 'tm', swap)  2.55 us
    ppermute x1, starting transfers between devices, two_steps(): far_lat = lax.ppermute(far_lat, 'lat', pairs[1])  1.91 us
    ppermute x1, starting transfers between devices, two_steps(): near_lat = lax.ppermute(near_lat, 'lat', pairs[0])  1.64 us
    ppermute x1, starting transfers between devices, two_steps(): far_sides = lax.ppermute(far_sides, 'lon', round_lon[1])  1.64 us
    ppermute x1, starting transfers between devices, two_steps(): edges = lax.ppermute(edges, 'tm', swap)  1.56 us
  transfers between devices with their start and end apart: 11, of which 5 were waited for; matrix products, arithmetic and copies ran while one was open for 0% of the time, Pallas kernels for 29%

commit v1 on v0

--- a/solution.py
+++ b/solution.py
@@ -392,8 +392,8 @@
     return y * (2.0 - d * y)
 
 
-def face(a, b):
-    return 2.0 * a * b * reciprocal(jnp.maximum(a + b, 1e-30))
+def face(a, b, twice):
+    return twice * b * reciprocal(jnp.maximum(a + b, 1e-30))
 
 
 def woven(ref, at):
@@ -443,10 +443,11 @@
         for u in range(width):
             at = start + u
             after = woven(K, at + 1)
-            side = face(here, after)
-            row = face(here, next_row(here))
+            twice = 2.0 * here
+            side = face(here, after, twice)
+            row = face(here, next_row(here), twice)
             previous = last_row(row)
-            level = jnp.where(inside, face(here, pltpu.roll(here, 127, 1)), 0.0)
+            level = jnp.where(inside, face(here, pltpu.roll(here, 127, 1), twice), 0.0)
             sums = (before + side) + (row + previous) + (level + pltpu.roll(level, 1, 1))
             wx[at], wy[at], wyp[at], wl[at] = side, row, previous, level
             total[at] = sums
@@ -570,11 +571,11 @@
 
     def step(q):
         for j in range(4):
-            rows = pl.ds(q + 4 * j, LEVELS, stride=ROWS)
-            value = it[rows, :]
+            row = q + 4 * j
+            value = it[pl.ds(row, LEVELS, stride=ROWS), :]
             for piece, quarter in ((own_low, 1 + t), (own_high, 3 * t), (got_low, 2 - t)):
                 value = jnp.where(group == quarter, value + placed(piece[q], j, quarter), value)
-            most[rows, :] = value
+            most[row] = value
 
     blocks(0, 4, 2, step)
 
@@ -592,9 +593,8 @@
         for q in range(4):
             value = got_high[q, pl.ds(pl.multiple_of(c * part, part), part), :]
             for j in range(4):
-                rows = pl.ds(c * part * ROWS + q + 4 * j, part, stride=ROWS)
-                old = most[rows, :]
-                out[rows, :] = jnp.where(here, old + placed(value, j, quarter), old)
+                old = most[q + 4 * j, pl.ds(pl.multiple_of(c * part, part), part), :]
+                out[pl.ds(c * part * ROWS + q + 4 * j, part, stride=ROWS), :] = jnp.where(here, old + placed(value, j, quarter), old)
         copy(c).start()
 
     blocks(0, CHUNKS, 1, step)
@@ -675,7 +675,7 @@
         functools.partial(iterate_half, 1), corrections, [*given, xs, edge], scratch=fields, limit=16
     )
     got_high = lax.ppermute(send_high, "tm", swap)
-    (most,) = call(finish_most, [shape(*flat)], [it, own_low, own_high, got_low])
+    (most,) = call(finish_most, [shape(ROWS, LEVELS, LONS)], [it, own_low, own_high, got_low])
     (out,) = call(
         finish,
         [shape(*flat)],

time: 36.5 us -> 36.5 us (level)
  no operation moved by 1% of the time
where the time goes in v1:
time: 36.5 us; the launch traced here: 36.3 us
  starting transfers between devices  14.1 us (39%)
  Pallas kernels  13.5 us (37%)
  waiting for transfers between devices  8.58 us (24%)
    pallas_call x12, Pallas kernels, call(): pl.pallas_call(body, out_shape=outs, in_specs=specs(len(ins), hbm_ins), o...  13.5 us
    ppermute x1, starting transfers between devices, two_steps(): far_rows = lax.ppermute(far_rows, 'lat', pairs[1])  3.64 us
    ppermute x1, waiting for transfers between devices, two_steps(): far_lat = lax.ppermute(far_lat, 'lat', pairs[1])  3.26 us
    ppermute x1, waiting for transfers between devices, two_steps(): got_high = lax.ppermute(send_high, 'tm', swap)  2.67 us
    ppermute x1, starting transfers between devices, two_steps(): far_lat = lax.ppermute(far_lat, 'lat', pairs[1])  1.91 us
    ppermute x1, starting transfers between devices, two_steps(): near_lat = lax.ppermute(near_lat, 'lat', pairs[0])  1.64 us
    ppermute x1, starting transfers between devices, two_steps(): far_sides = lax.ppermute(far_sides, 'lon', round_lon[1])  1.64 us
    ppermute x1, starting transfers between devices, two_steps(): edges = lax.ppermute(edges, 'tm', swap)  1.56 us
  transfers between devices with their start and end apart: 11, of which 5 were waited for; matrix products, arithmetic and copies ran while one was open for 0% of the time, Pallas kernels for 29%

profile of v1, /device:TPU:16, one launch (start us, length us, event | category | flops | bytes accessed | tf_op | source)
XLA Modules:
  0.0 36.3 jit_solution(11875971015423176892)
XLA Ops:
  0.0 1.9 %shard_map.55 = (f32[68,8,128]{2,1,0:T(8,128)S(1)}, f32[68,8,128]{2,1,0:T(8,128)S(1)}, f32[2048,128]{1,0:T(8,128)S(1)}, f32[1024,128]{1,0:T(8,128)S(1)}) custom-call(f32[64,16,128]{2,1,0:T(8,128)} %bitcast.11, f32[64,16,128]{2,1,0:T(8,128)} %bitcast.12), custom_call_target="tpu_custom_call" | custom-call | flops 12713984 | bytes 3178496 | tf_op jit(solution)/shard_map/pallas_call | solution.py:140
  1.9 1.6 %collective-permute-start.4 = (f32[68,8,128]{2,1,0:T(8,128)S(1)}, f32[68,8,128]{2,1,0:T(8,128)S(1)}, u32[]{:S(2)}, u32[]{:S(2)}) collective-permute-start(f32[68,8,128]{2,1,0:T(8,128)S(1)} %get-tuple-element.43), channel_id=1, source_target_pairs={{0,16},{16,0},{1,17},{17,1},{2,18},{18,2},{3,19},{19,3},{4,20},{20... | collective-permute-start | bytes 835592 | tf_op jit(solution)/shard_map/ppermute | solution.py:628
  3.5 1.5 %shard_map.56 = (f32[2048,128]{1,0:T(8,128)S(1)}, f32[6,16,128]{2,1,0:T(8,128)S(1)}, f32[6,16,128]{2,1,0:T(8,128)S(1)}) custom-call(f32[2048,128]{1,0:T(8,128)S(1)} %get-tuple-element.36.turned, s32[1024,128]{1,0:T(8,128)S(1)} %bitcast.9, f32[1024,128]{1,0:T(8,128)S(1)} %bitcast.10, f32[8]{0:T(128)} %table_hbm.1), custom_call_target="tpu_custom_call" | custom-call | flops 12976256 | bytes 3244064 | tf_op jit(solution)/shard_map/pallas_call | solution.py:140
  5.0 0.1 collective-permute-start
  5.1 1.6 %collective-permute-start.1 = (f32[6,16,128]{2,1,0:T(8,128)S(1)}, f32[6,16,128]{2,1,0:T(8,128)S(1)}, u32[]{:S(2)}, u32[]{:S(2)}) collective-permute-start(f32[6,16,128]{2,1,0:T(8,128)S(1)} %get-tuple-element.39), channel_id=1, source_target_pairs={{4,8},{12,0},{8,4},{0,12},{5,9},{13,1},{9,5},{1,13},{6,10},{14,2},... | collective-permute-start | bytes 147464 | tf_op jit(solution)/shard_map/ppermute | solution.py:639
  6.7 0.5 %collective-permute-start.5 = (f32[68,8,128]{2,1,0:T(8,128)S(1)}, f32[68,8,128]{2,1,0:T(8,128)S(1)}, u32[]{:S(2)}, u32[]{:S(2)}) collective-permute-start(f32[68,8,128]{2,1,0:T(8,128)S(1)} %get-tuple-element.46), channel_id=1, source_target_pairs={{0,16},{16,0},{1,17},{17,1},{2,18},{18,2},{3,19},{19,3},{4,20},{20... | collective-permute-start | bytes 835592 | tf_op jit(solution)/shard_map/ppermute | solution.py:629
  7.2 0.0 collective-permute-done.near_sides
  7.2 1.4 %collective-permute-done.1.far_sides = f32[6,16,128]{2,1,0:T(8,128)S(1)} collective-permute-done((f32[6,16,128]{2,1,0:T(8,128)S(1)}, f32[6,16,128]{2,1,0:T(8,128)S(1)}, u32[]{:S(2)}, u32[]{:S(2)}) %collective-permute-start.1) | collective-permute-done | bytes 49184 | tf_op jit(solution)/shard_map/ppermute | solution.py:639
  8.6 0.4 %shard_map.57 = (f32[72,16,128]{2,1,0:T(8,128)S(1)}, f32[72,16,128]{2,1,0:T(8,128)S(1)}, f32[46,8,128]{2,1,0:T(8,128)S(1)}, f32[46,8,128]{2,1,0:T(8,128)S(1)}, f32[4,16,128]{2,1,0:T(8,128)S(1)}) custom-call(f32[128,16,128]{2,1,0:T(8,128)S(1)} %bitcast.7, f32[128,16,128]{2,1,0:T(8,128)S(1)} %bitcast.8, f32[6,16,128]{2,1,0:T(8,128)S(1)} %collective-permute-done.near_sides, ...), custom_call_target="tpu_custom_call" | custom-call | flops 15138816 | bytes 3784704 | tf_op jit(solution)/shard_map/pallas_call | solution.py:140
  9.1 1.6 %collective-permute-start.2 = (f32[46,8,128]{2,1,0:T(8,128)S(1)}, f32[46,8,128]{2,1,0:T(8,128)S(1)}, u32[]{:S(2)}, u32[]{:S(2)}) collective-permute-start(f32[46,8,128]{2,1,0:T(8,128)S(1)} %get-tuple-element.41), channel_id=1, source_target_pairs={{0,1},{2,3},{1,0},{3,2},{4,5},{6,7},{5,4},{7,6},{8,9},{10,11},{9,8... | collective-permute-start | bytes 565256 | tf_op jit(solution)/shard_map/ppermute | solution.py:647
  10.7 1.9 %collective-permute-start.3 = (f32[46,8,128]{2,1,0:T(8,128)S(1)}, f32[46,8,128]{2,1,0:T(8,128)S(1)}, u32[]{:S(2)}, u32[]{:S(2)}) collective-permute-start(f32[46,8,128]{2,1,0:T(8,128)S(1)} %get-tuple-element.42), channel_id=1, source_target_pairs={{1,2},{2,1},{5,6},{6,5},{9,10},{10,9},{13,14},{14,13},{17,18},{18,... | collective-permute-start | bytes 565256 | tf_op jit(solution)/shard_map/ppermute | solution.py:648
  12.6 0.0 collective-permute-done.4.edges
  12.6 0.2 shard_map.58
  12.8 0.4 collective-permute-start.6
  13.2 3.6 %collective-permute-start.7 = (f32[44,8,128]{2,1,0:T(8,128)S(1)}, f32[44,8,128]{2,1,0:T(8,128)S(1)}, u32[]{:S(2)}, u32[]{:S(2)}) collective-permute-start(f32[44,8,128]{2,1,0:T(8,128)S(1)} %get-tuple-element.55), channel_id=1, source_target_pairs={{1,2},{2,1},{5,6},{6,5},{9,10},{10,9},{13,14},{14,13},{17,18},{18,... | collective-permute-start | bytes 540680 | tf_op jit(solution)/shard_map/ppermute | solution.py:652
  16.8 0.0 collective-permute-done.2.near_lat
  16.8 3.3 %collective-permute-done.3.far_lat = f32[46,8,128]{2,1,0:T(8,128)S(1)} collective-permute-done((f32[46,8,128]{2,1,0:T(8,128)S(1)}, f32[46,8,128]{2,1,0:T(8,128)S(1)}, u32[]{:S(2)}, u32[]{:S(2)}) %collective-permute-start.3) | collective-permute-done | bytes 188448 | tf_op jit(solution)/shard_map/ppermute | solution.py:648
  20.1 0.6 %collective-permute-start.8 = (f32[4,24,128]{2,1,0:T(8,128)S(1)}, f32[4,24,128]{2,1,0:T(8,128)S(1)}, u32[]{:S(2)}, u32[]{:S(2)}) collective-permute-start(f32[4,24,128]{2,1,0:T(8,128)S(1)} %shard_map.63), channel_id=1, source_target_pairs={{0,16},{16,0},{1,17},{17,1},{2,18},{18,2},{3,19},{19,3},{4,20},{20... | collective-permute-start | bytes 147464 | tf_op jit(solution)/shard_map/ppermute | solution.py:655
  20.7 0.0 collective-permute-done.5.middle
  20.7 0.6 %shard_map.59 = (f32[72,16,128]{2,1,0:T(8,128)S(1)}, f32[72,16,128]{2,1,0:T(8,128)S(1)}) custom-call(f32[68,8,128]{2,1,0:T(8,128)S(1)} %get-tuple-element.45.edges, f32[68,8,128]{2,1,0:T(8,128)S(1)} %collective-permute-done.5.middle, f32[72,16,128]{2,1,0:T(8,128)S(1)} %get-tuple-element.44.own, f32[72,16,128]{2,1,0:T(8,128)S(1)} %get-tuple-element.40.own_fixed), custom_call_target="tpu_custom_call" | custom-call | flops 11665408 | bytes 2916352 | tf_op jit(solution)/shard_map/pallas_call | solution.py:140
  21.3 1.6 %shard_map.60 = (f32[72,24,128]{2,1,0:T(8,128)S(1)}, f32[72,24,128]{2,1,0:T(8,128)S(1)}, f32[72,24,128]{2,1,0:T(8,128)S(1)}, f32[72,24,128]{2,1,0:T(8,128)S(1)},...) custom-call(f32[72,16,128]{2,1,0:T(8,128)S(1)} %get-tuple-element.40.own_fixed, ...), custom_call_target="tpu_custom_call" | custom-call | flops 27459584 | bytes 6864896 | tf_op jit(solution)/shard_map/pallas_call | solution.py:140
  22.9 0.0 collective-permute-done.6.near_rows
  22.9 0.6 %collective-permute-done.7.far_rows = f32[44,8,128]{2,1,0:T(8,128)S(1)} collective-permute-done((f32[44,8,128]{2,1,0:T(8,128)S(1)}, f32[44,8,128]{2,1,0:T(8,128)S(1)}, u32[]{:S(2)}, u32[]{:S(2)}) %collective-permute-start.7) | collective-permute-done | bytes 180256 | tf_op jit(solution)/shard_map/ppermute | solution.py:652
  23.5 0.2 shard_map.61
  23.7 3.1 %shard_map.62 = (f32[4,64,128]{2,1,0:T(8,128)S(1)}, f32[4,64,128]{2,1,0:T(8,128)S(1)}, f32[12,24,128]{2,1,0:T(8,128)S(1)}) custom-call(f32[72,24,128]{2,1,0:T(8,128)S(1)} %get-tuple-element.48.wx, f32[72,24,128]{2,1,0:T(8,128)S(1)} %get-tuple-element.49.wy, f32[72,24,128]{2,1,0:T(8,128)S(1)} %get-tuple-element.50.wyp, ...), custom_call_target="tpu_custom_call" | custom-call | flops 32309248 | bytes 8077312 | tf_op jit(solution)/shard_map/pallas_call | solution.py:140
  26.8 0.9 %collective-permute-start.9 = (f32[4,64,128]{2,1,0:T(8,128)S(1)}, f32[4,64,128]{2,1,0:T(8,128)S(1)}, u32[]{:S(2)}, u32[]{:S(2)}) collective-permute-start(f32[4,64,128]{2,1,0:T(8,128)S(1)} %get-tuple-element.63), channel_id=1, source_target_pairs={{0,16},{16,0},{1,17},{17,1},{2,18},{18,2},{3,19},{19,3},{4,20},{20... | collective-permute-start | bytes 393224 | tf_op jit(solution)/shard_map/ppermute | solution.py:673
  27.7 2.4 %shard_map.64 = (f32[4,64,128]{2,1,0:T(8,128)S(1)}, f32[4,64,128]{2,1,0:T(8,128)S(1)}) custom-call(f32[72,24,128]{2,1,0:T(8,128)S(1)} %get-tuple-element.48.wx, f32[72,24,128]{2,1,0:T(8,128)S(1)} %get-tuple-element.49.wy, f32[72,24,128]{2,1,0:T(8,128)S(1)} %get-tuple-element.50.wyp, f32[72,24,128]{2,1,0:T(8,128)S(1)} %get-tuple-element.51.wl, ...), custom_call_target="tpu_custom_call" | custom-call | flops 32505856 | bytes 8126464 | tf_op jit(solution)/shard_map/pallas_call | solution.py:140
  30.1 1.2 %collective-permute-start.10 = (f32[4,64,128]{2,1,0:T(8,128)S(1)}, f32[4,64,128]{2,1,0:T(8,128)S(1)}, u32[]{:S(2)}, u32[]{:S(2)}) collective-permute-start(f32[4,64,128]{2,1,0:T(8,128)S(1)} %get-tuple-element.64), channel_id=1, source_target_pairs={{0,16},{16,0},{1,17},{17,1},{2,18},{18,2},{3,19},{19,3},{4,20},{20... | collective-permute-start | bytes 393224 | tf_op jit(solution)/shard_map/ppermute | solution.py:677
  31.3 0.6 %collective-permute-done.9.got_low = f32[4,64,128]{2,1,0:T(8,128)S(1)} collective-permute-done((f32[4,64,128]{2,1,0:T(8,128)S(1)}, f32[4,64,128]{2,1,0:T(8,128)S(1)}, u32[]{:S(2)}, u32[]{:S(2)}) %collective-permute-start.9) | collective-permute-done | bytes 131104 | tf_op jit(solution)/shard_map/ppermute | solution.py:673
  31.9 0.5 %shard_map.65.most = f32[16,64,128]{2,1,0:T(8,128)S(1)} custom-call(f32[1024,128]{1,0:T(8,128)S(1)} %get-tuple-element.35.it, f32[4,64,128]{2,1,0:T(8,128)S(1)} %get-tuple-element.59.own_low, f32[4,64,128]{2,1,0:T(8,128)S(1)} %get-tuple-element.62.own_high, f32[4,64,128]{2,1,0:T(8,128)S(1)} %collective-permute-done.9.got_low), custom_call_target="tpu_custom_call" | custom-call | flops 5767168 | bytes 1441792 | tf_op jit(solution)/shard_map/pallas_call | solution.py:140
  32.5 2.7 %collective-permute-done.10.got_high = f32[4,64,128]{2,1,0:T(8,128)S(1)} collective-permute-done((f32[4,64,128]{2,1,0:T(8,128)S(1)}, f32[4,64,128]{2,1,0:T(8,128)S(1)}, u32[]{:S(2)}, u32[]{:S(2)}) %collective-permute-start.10) | collective-permute-done | bytes 131104 | tf_op jit(solution)/shard_map/ppermute | solution.py:677
  35.2 1.1 %shard_map.66 = f32[1024,128]{1,0:T(8,128)} custom-call(f32[16,64,128]{2,1,0:T(8,128)S(1)} %shard_map.65.most, f32[4,64,128]{2,1,0:T(8,128)S(1)} %collective-permute-done.10.got_high), custom_call_target="tpu_custom_call" | custom-call | flops 4718592 | bytes 1179648 | tf_op jit(solution)/shard_map/pallas_call | solution.py:140
  (6 shorter events, 0.0 us)
Async XLA Ops:
  0.0 3.5 %copy-start = (s32[64,16,128]{2,1,0:T(8,128)S(1)}, s32[64,16,128]{2,1,0:T(8,128)}, u32[]{:S(2)}) copy-start(s32[64,16,128]{2,1,0:T(8,128)} %param.8) | copy-start | bytes 1572868
  0.0 3.5 %copy-start.1 = (f32[64,16,128]{2,1,0:T(8,128)S(1)}, f32[64,16,128]{2,1,0:T(8,128)}, u32[]{:S(2)}) copy-start(f32[64,16,128]{2,1,0:T(8,128)} %param.7) | copy-start | bytes 1572868
  1.9 10.7 %collective-permute-start.4 = (f32[68,8,128]{2,1,0:T(8,128)S(1)}, f32[68,8,128]{2,1,0:T(8,128)S(1)}, u32[]{:S(2)}, u32[]{:S(2)}) collective-permute-start(f32[68,8,128]{2,1,0:T(8,128)S(1)} %get-tuple-element.43), channel_id=1, source_target_pairs={{0,16},{16,0},{1,17},{17,1},{2,18},{18,2},{3,19},{19,3},{4,20},{20... | collective-permute-start | bytes 835592 | tf_op jit(solution)/shard_map/ppermute | solution.py:628
  5.0 2.3 %collective-permute-start = (f32[6,16,128]{2,1,0:T(8,128)S(1)}, f32[6,16,128]{2,1,0:T(8,128)S(1)}, u32[]{:S(2)}, u32[]{:S(2)}) collective-permute-start(f32[6,16,128]{2,1,0:T(8,128)S(1)} %get-tuple-element.38), channel_id=1, source_target_pairs={{0,4},{8,12},{4,0},{12,8},{1,5},{9,13},{5,1},{13,9},{2,6},{10,14},... | collective-permute-start | bytes 147464 | tf_op jit(solution)/shard_map/ppermute | solution.py:638
  5.1 3.6 %collective-permute-start.1 = (f32[6,16,128]{2,1,0:T(8,128)S(1)}, f32[6,16,128]{2,1,0:T(8,128)S(1)}, u32[]{:S(2)}, u32[]{:S(2)}) collective-permute-start(f32[6,16,128]{2,1,0:T(8,128)S(1)} %get-tuple-element.39), channel_id=1, source_target_pairs={{4,8},{12,0},{8,4},{0,12},{5,9},{13,1},{9,5},{1,13},{6,10},{14,2},... | collective-permute-start | bytes 147464 | tf_op jit(solution)/shard_map/ppermute | solution.py:639
  6.7 14.0 %collective-permute-start.5 = (f32[68,8,128]{2,1,0:T(8,128)S(1)}, f32[68,8,128]{2,1,0:T(8,128)S(1)}, u32[]{:S(2)}, u32[]{:S(2)}) collective-permute-start(f32[68,8,128]{2,1,0:T(8,128)S(1)} %get-tuple-element.46), channel_id=1, source_target_pairs={{0,16},{16,0},{1,17},{17,1},{2,18},{18,2},{3,19},{19,3},{4,20},{20... | collective-permute-start | bytes 835592 | tf_op jit(solution)/shard_map/ppermute | solution.py:629
  9.1 7.8 %collective-permute-start.2 = (f32[46,8,128]{2,1,0:T(8,128)S(1)}, f32[46,8,128]{2,1,0:T(8,128)S(1)}, u32[]{:S(2)}, u32[]{:S(2)}) collective-permute-start(f32[46,8,128]{2,1,0:T(8,128)S(1)} %get-tuple-element.41), channel_id=1, source_target_pairs={{0,1},{2,3},{1,0},{3,2},{4,5},{6,7},{5,4},{7,6},{8,9},{10,11},{9,8... | collective-permute-start | bytes 565256 | tf_op jit(solution)/shard_map/ppermute | solution.py:647
  10.7 9.4 %collective-permute-start.3 = (f32[46,8,128]{2,1,0:T(8,128)S(1)}, f32[46,8,128]{2,1,0:T(8,128)S(1)}, u32[]{:S(2)}, u32[]{:S(2)}) collective-permute-start(f32[46,8,128]{2,1,0:T(8,128)S(1)} %get-tuple-element.42), channel_id=1, source_target_pairs={{1,2},{2,1},{5,6},{6,5},{9,10},{10,9},{13,14},{14,13},{17,18},{18,... | collective-permute-start | bytes 565256 | tf_op jit(solution)/shard_map/ppermute | solution.py:648
  12.8 10.1 %collective-permute-start.6 = (f32[44,8,128]{2,1,0:T(8,128)S(1)}, f32[44,8,128]{2,1,0:T(8,128)S(1)}, u32[]{:S(2)}, u32[]{:S(2)}) collective-permute-start(f32[44,8,128]{2,1,0:T(8,128)S(1)} %get-tuple-element.54), channel_id=1, source_target_pairs={{0,1},{2,3},{1,0},{3,2},{4,5},{6,7},{5,4},{7,6},{8,9},{10,11},{9,8... | collective-permute-start | bytes 540680 | tf_op jit(solution)/shard_map/ppermute | solution.py:651
  13.2 10.3 %collective-permute-start.7 = (f32[44,8,128]{2,1,0:T(8,128)S(1)}, f32[44,8,128]{2,1,0:T(8,128)S(1)}, u32[]{:S(2)}, u32[]{:S(2)}) collective-permute-start(f32[44,8,128]{2,1,0:T(8,128)S(1)} %get-tuple-element.55), channel_id=1, source_target_pairs={{1,2},{2,1},{5,6},{6,5},{9,10},{10,9},{13,14},{14,13},{17,18},{18,... | collective-permute-start | bytes 540680 | tf_op jit(solution)/shard_map/ppermute | solution.py:652
  20.1 7.6 %collective-permute-start.8 = (f32[4,24,128]{2,1,0:T(8,128)S(1)}, f32[4,24,128]{2,1,0:T(8,128)S(1)}, u32[]{:S(2)}, u32[]{:S(2)}) collective-permute-start(f32[4,24,128]{2,1,0:T(8,128)S(1)} %shard_map.63), channel_id=1, source_target_pairs={{0,16},{16,0},{1,17},{17,1},{2,18},{18,2},{3,19},{19,3},{4,20},{20... | collective-permute-start | bytes 147464 | tf_op jit(solution)/shard_map/ppermute | solution.py:655
  26.8 5.2 %collective-permute-start.9 = (f32[4,64,128]{2,1,0:T(8,128)S(1)}, f32[4,64,128]{2,1,0:T(8,128)S(1)}, u32[]{:S(2)}, u32[]{:S(2)}) collective-permute-start(f32[4,64,128]{2,1,0:T(8,128)S(1)} %get-tuple-element.63), channel_id=1, source_target_pairs={{0,16},{16,0},{1,17},{17,1},{2,18},{18,2},{3,19},{19,3},{4,20},{20... | collective-permute-start | bytes 393224 | tf_op jit(solution)/shard_map/ppermute | solution.py:673
  30.1 5.0 %collective-permute-start.10 = (f32[4,64,128]{2,1,0:T(8,128)S(1)}, f32[4,64,128]{2,1,0:T(8,128)S(1)}, u32[]{:S(2)}, u32[]{:S(2)}) collective-permute-start(f32[4,64,128]{2,1,0:T(8,128)S(1)} %get-tuple-element.64), channel_id=1, source_target_pairs={{0,16},{16,0},{1,17},{17,1},{2,18},{18,2},{3,19},{19,3},{4,20},{20... | collective-permute-start | bytes 393224 | tf_op jit(solution)/shard_map/ppermute | solution.py:677

commit v2 on v1

--- a/solution.py
+++ b/solution.py
@@ -125,7 +125,7 @@
 PAIRS = PLACES // 2
 SENT_PAIRS = SENT // 2
 QUADS = PLACES // 4
-SPLIT = 26
+SPLIT = 24
 FIXED = SPLIT
 PARTNER = SPLIT + QUADS
 CHUNKS = 4
@@ -135,8 +135,8 @@
     return [pl.BlockSpec(memory_space=pltpu.HBM if i in hbm else pltpu.VMEM) for i in range(count)]
 
 
-def call(body, outs, ins, scratch=(), limit=8, hbm_ins=(), hbm_outs=()):
-    moved = sum(x.size * 4 for x in ins) + sum(x.size * 4 for x in outs)
+def call(body, outs, ins, scratch=(), limit=8, hbm_ins=(), hbm_outs=(), work=1):
+    moved = work * (sum(x.size * 4 for x in ins) + sum(x.size * 4 for x in outs))
     return pl.pallas_call(
         body,
         out_shape=outs,
@@ -304,7 +304,7 @@
     def rows(i):
         near_lat[i], far_lat[i] = edge_pair(own[i], own[i + PAIRS])
 
-    blocks(0, SPLIT, 13, rows)
+    blocks(0, SPLIT, 12, rows)
     low = in_low(TILE)
 
     def fixed_rows(i):
@@ -337,20 +337,20 @@
     def rest(i):
         near_rows[SENT_PAIRS + i], far_rows[SENT_PAIRS + i] = edge_pair(own[SPLIT + i], own[SPLIT + i + PAIRS])
 
-    blocks(0, PAIRS - SPLIT, 10, rest)
+    blocks(0, PAIRS - SPLIT, 12, rest)
 
 
 def join(near_lat, far_lat, near_rows, far_rows, halo, other):
     def place(i, tiles):
         halo[i], halo[i + PAIRS] = tiles
 
-    blocks(0, SPLIT, 13, lambda i: place(i, halo_tiles(near_lat[i], far_lat[i])))
+    blocks(0, SPLIT, 12, lambda i: place(i, halo_tiles(near_lat[i], far_lat[i])))
 
     def rest(i):
         at = SENT_PAIRS + i
         place(SPLIT + i, halo_tiles(near_rows[at], far_rows[at]))
 
-    blocks(0, PAIRS - SPLIT, 10, rest)
+    blocks(0, PAIRS - SPLIT, 12, rest)
 
     def theirs(i):
         other[main_at(i)], other[main_at(i + SENT_PAIRS)] = halo_tiles(near_rows[i], far_rows[i])
@@ -380,7 +380,7 @@
     blocks(0, SENT, 17, step)
 
 
-def strips(partner, near_lat, far_lat, xs):
+def strips(partner, near_lat, far_lat, _, xs):
     for i in range(2):
         at = PARTNER + i
         for place, tile in zip((i, i + 2), halo_tiles(near_lat[at], far_lat[at])):
@@ -647,11 +647,13 @@
     near_lat = lax.ppermute(near_lat, "lat", pairs[0])
     far_lat = lax.ppermute(far_lat, "lat", pairs[1])
     rows = shape(SENT_PAIRS + PAIRS - SPLIT, TILE, 128)
-    edges, near_rows, far_rows = call(pass_rows, [half_rows, rows, rows], [edges, own_main, own_fixed])
+    edges, near_rows, far_rows = call(
+        pass_rows, [half_rows, rows, rows], [edges, own_main, own_fixed], work=200
+    )
     near_rows = lax.ppermute(near_rows, "lat", pairs[0])
     far_rows = lax.ppermute(far_rows, "lat", pairs[1])
     it_main, source_main = call(gather, [main, main], [edges, middle, own_main, own_fixed])
-    (xs,) = call(strips, [shape(HALO, ROWS + TILE, 128)], [partner, near_lat, far_lat])
+    (xs,) = call(strips, [shape(HALO, ROWS + TILE, 128)], [partner, near_lat, far_lat, it_main])
     xs = lax.ppermute(xs, "tm", swap)
     ready = call(
         prepare,

time: 36.5 us -> 36.1 us (0.989)
    ppermute x1, waiting for transfers between devices: 3.26 us -> 2.46 us  [two_steps(): far_lat = lax.ppermute(far_lat, 'lat', pairs[1])]
    ppermute x1, waiting for transfers between devices: 0.63 us -> 1.41 us  [two_steps(): far_rows = lax.ppermute(far_rows, 'lat', pairs[1])]
where the time goes in v2:
time: 36.1 us; the launch traced here: 35.9 us
  starting transfers between devices  14.1 us (39%)
  Pallas kernels  13.5 us (37%)
  waiting for transfers between devices  8.22 us (23%)
    pallas_call x12, Pallas kernels, call(): pl.pallas_call(body, out_shape=outs, in_specs=specs(len(ins), hbm_ins), o...  13.5 us
    ppermute x1, starting transfers between devices, two_steps(): far_rows = lax.ppermute(far_rows, 'lat', pairs[1])  3.64 us
    ppermute x1, waiting for transfers between devices, two_steps(): far_lat = lax.ppermute(far_lat, 'lat', pairs[1])  2.46 us
    ppermute x1, waiting for transfers between devices, two_steps(): got_high = lax.ppermute(send_high, 'tm', swap)  2.32 us
    ppermute x1, starting transfers between devices, two_steps(): far_lat = lax.ppermute(far_lat, 'lat', pairs[1])  1.91 us
    ppermute x1, starting transfers between devices, two_steps(): near_lat = lax.ppermute(near_lat, 'lat', pairs[0])  1.64 us
    ppermute x1, starting transfers between devices, two_steps(): far_sides = lax.ppermute(far_sides, 'lon', round_lon[1])  1.64 us
    ppermute x1, starting transfers between devices, two_steps(): edges = lax.ppermute(edges, 'tm', swap)  1.56 us
  transfers between devices with their start and end apart: 11, of which 5 were waited for; matrix products, arithmetic and copies ran while one was open for 0% of the time, Pallas kernels for 29%

profile of v2, /device:TPU:16, one launch (start us, length us, event | category | flops | bytes accessed | tf_op | source)
XLA Modules:
  0.0 35.9 jit_solution(1875772545084488953)
XLA Ops:
  0.0 1.9 %shard_map.55 = (f32[68,8,128]{2,1,0:T(8,128)S(1)}, f32[68,8,128]{2,1,0:T(8,128)S(1)}, f32[2048,128]{1,0:T(8,128)S(1)}, f32[1024,128]{1,0:T(8,128)S(1)}) custom-call(f32[64,16,128]{2,1,0:T(8,128)} %bitcast.11, f32[64,16,128]{2,1,0:T(8,128)} %bitcast.12), custom_call_target="tpu_custom_call" | custom-call | flops 12713984 | bytes 3178496 | tf_op jit(solution)/shard_map/pallas_call | solution.py:140
  1.9 1.6 %collective-permute-start.4 = (f32[68,8,128]{2,1,0:T(8,128)S(1)}, f32[68,8,128]{2,1,0:T(8,128)S(1)}, u32[]{:S(2)}, u32[]{:S(2)}) collective-permute-start(f32[68,8,128]{2,1,0:T(8,128)S(1)} %get-tuple-element.43), channel_id=1, source_target_pairs={{0,16},{16,0},{1,17},{17,1},{2,18},{18,2},{3,19},{19,3},{4,20},{20... | collective-permute-start | bytes 835592 | tf_op jit(solution)/shard_map/ppermute | solution.py:628
  3.5 1.5 %shard_map.56 = (f32[2048,128]{1,0:T(8,128)S(1)}, f32[6,16,128]{2,1,0:T(8,128)S(1)}, f32[6,16,128]{2,1,0:T(8,128)S(1)}) custom-call(f32[2048,128]{1,0:T(8,128)S(1)} %get-tuple-element.36.turned, s32[1024,128]{1,0:T(8,128)S(1)} %bitcast.9, f32[1024,128]{1,0:T(8,128)S(1)} %bitcast.10, f32[8]{0:T(128)} %table_hbm.1), custom_call_target="tpu_custom_call" | custom-call | flops 12976256 | bytes 3244064 | tf_op jit(solution)/shard_map/pallas_call | solution.py:140
  5.0 0.1 collective-permute-start
  5.1 1.6 %collective-permute-start.1 = (f32[6,16,128]{2,1,0:T(8,128)S(1)}, f32[6,16,128]{2,1,0:T(8,128)S(1)}, u32[]{:S(2)}, u32[]{:S(2)}) collective-permute-start(f32[6,16,128]{2,1,0:T(8,128)S(1)} %get-tuple-element.39), channel_id=1, source_target_pairs={{4,8},{12,0},{8,4},{0,12},{5,9},{13,1},{9,5},{1,13},{6,10},{14,2},... | collective-permute-start | bytes 147464 | tf_op jit(solution)/shard_map/ppermute | solution.py:639
  6.7 0.5 %collective-permute-start.5 = (f32[68,8,128]{2,1,0:T(8,128)S(1)}, f32[68,8,128]{2,1,0:T(8,128)S(1)}, u32[]{:S(2)}, u32[]{:S(2)}) collective-permute-start(f32[68,8,128]{2,1,0:T(8,128)S(1)} %get-tuple-element.46), channel_id=1, source_target_pairs={{0,16},{16,0},{1,17},{17,1},{2,18},{18,2},{3,19},{19,3},{4,20},{20... | collective-permute-start | bytes 835592 | tf_op jit(solution)/shard_map/ppermute | solution.py:629
  7.2 0.0 collective-permute-done.near_sides
  7.2 1.4 %collective-permute-done.1.far_sides = f32[6,16,128]{2,1,0:T(8,128)S(1)} collective-permute-done((f32[6,16,128]{2,1,0:T(8,128)S(1)}, f32[6,16,128]{2,1,0:T(8,128)S(1)}, u32[]{:S(2)}, u32[]{:S(2)}) %collective-permute-start.1) | collective-permute-done | bytes 49184 | tf_op jit(solution)/shard_map/ppermute | solution.py:639
  8.6 0.4 %shard_map.57 = (f32[72,16,128]{2,1,0:T(8,128)S(1)}, f32[72,16,128]{2,1,0:T(8,128)S(1)}, f32[44,8,128]{2,1,0:T(8,128)S(1)}, f32[44,8,128]{2,1,0:T(8,128)S(1)}, f32[4,16,128]{2,1,0:T(8,128)S(1)}) custom-call(f32[128,16,128]{2,1,0:T(8,128)S(1)} %bitcast.7, f32[128,16,128]{2,1,0:T(8,128)S(1)} %bitcast.8, f32[6,16,128]{2,1,0:T(8,128)S(1)} %collective-permute-done.near_sides, ...), custom_call_target="tpu_custom_call" | custom-call | flops 15073280 | bytes 3768320 | tf_op jit(solution)/shard_map/pallas_call | solution.py:140
  9.0 1.6 %collective-permute-start.2 = (f32[44,8,128]{2,1,0:T(8,128)S(1)}, f32[44,8,128]{2,1,0:T(8,128)S(1)}, u32[]{:S(2)}, u32[]{:S(2)}) collective-permute-start(f32[44,8,128]{2,1,0:T(8,128)S(1)} %get-tuple-element.41), channel_id=1, source_target_pairs={{0,1},{2,3},{1,0},{3,2},{4,5},{6,7},{5,4},{7,6},{8,9},{10,11},{9,8... | collective-permute-start | bytes 540680 | tf_op jit(solution)/shard_map/ppermute | solution.py:647
  10.7 1.9 %collective-permute-start.3 = (f32[44,8,128]{2,1,0:T(8,128)S(1)}, f32[44,8,128]{2,1,0:T(8,128)S(1)}, u32[]{:S(2)}, u32[]{:S(2)}) collective-permute-start(f32[44,8,128]{2,1,0:T(8,128)S(1)} %get-tuple-element.42), channel_id=1, source_target_pairs={{1,2},{2,1},{5,6},{6,5},{9,10},{10,9},{13,14},{14,13},{17,18},{18,... | collective-permute-start | bytes 540680 | tf_op jit(solution)/shard_map/ppermute | solution.py:648
  12.6 0.0 collective-permute-done.4.edges
  12.6 0.2 shard_map.58
  12.8 0.4 %collective-permute-start.6 = (f32[46,8,128]{2,1,0:T(8,128)S(1)}, f32[46,8,128]{2,1,0:T(8,128)S(1)}, u32[]{:S(2)}, u32[]{:S(2)}) collective-permute-start(f32[46,8,128]{2,1,0:T(8,128)S(1)} %get-tuple-element.54), channel_id=1, source_target_pairs={{0,1},{2,3},{1,0},{3,2},{4,5},{6,7},{5,4},{7,6},{8,9},{10,11},{9,8... | collective-permute-start | bytes 565256 | tf_op jit(solution)/shard_map/ppermute | solution.py:653
  13.2 3.6 %collective-permute-start.7 = (f32[46,8,128]{2,1,0:T(8,128)S(1)}, f32[46,8,128]{2,1,0:T(8,128)S(1)}, u32[]{:S(2)}, u32[]{:S(2)}) collective-permute-start(f32[46,8,128]{2,1,0:T(8,128)S(1)} %get-tuple-element.55), channel_id=1, source_target_pairs={{1,2},{2,1},{5,6},{6,5},{9,10},{10,9},{13,14},{14,13},{17,18},{18,... | collective-permute-start | bytes 565256 | tf_op jit(solution)/shard_map/ppermute | solution.py:654
  16.8 0.0 collective-permute-done.5.middle
  16.8 0.6 %shard_map.59 = (f32[72,16,128]{2,1,0:T(8,128)S(1)}, f32[72,16,128]{2,1,0:T(8,128)S(1)}) custom-call(f32[68,8,128]{2,1,0:T(8,128)S(1)} %get-tuple-element.45.edges, f32[68,8,128]{2,1,0:T(8,128)S(1)} %collective-permute-done.5.middle, f32[72,16,128]{2,1,0:T(8,128)S(1)} %get-tuple-element.44.own, f32[72,16,128]{2,1,0:T(8,128)S(1)} %get-tuple-element.40.own_fixed), custom_call_target="tpu_custom_call" | custom-call | flops 11665408 | bytes 2916352 | tf_op jit(solution)/shard_map/pallas_call | solution.py:140
  17.5 2.5 %collective-permute-done.3.far_lat = f32[44,8,128]{2,1,0:T(8,128)S(1)} collective-permute-done((f32[44,8,128]{2,1,0:T(8,128)S(1)}, f32[44,8,128]{2,1,0:T(8,128)S(1)}, u32[]{:S(2)}, u32[]{:S(2)}) %collective-permute-start.3) | collective-permute-done | bytes 180256 | tf_op jit(solution)/shard_map/ppermute | solution.py:648
  19.9 0.6 %collective-permute-start.8 = (f32[4,24,128]{2,1,0:T(8,128)S(1)}, f32[4,24,128]{2,1,0:T(8,128)S(1)}, u32[]{:S(2)}, u32[]{:S(2)}) collective-permute-start(f32[4,24,128]{2,1,0:T(8,128)S(1)} %shard_map.63), channel_id=1, source_target_pairs={{0,16},{16,0},{1,17},{17,1},{2,18},{18,2},{3,19},{19,3},{4,20},{20... | collective-permute-start | bytes 147464 | tf_op jit(solution)/shard_map/ppermute | solution.py:657
  20.5 1.6 %shard_map.60 = (f32[72,24,128]{2,1,0:T(8,128)S(1)}, f32[72,24,128]{2,1,0:T(8,128)S(1)}, f32[72,24,128]{2,1,0:T(8,128)S(1)}, f32[72,24,128]{2,1,0:T(8,128)S(1)},...) custom-call(f32[72,16,128]{2,1,0:T(8,128)S(1)} %get-tuple-element.40.own_fixed, ...), custom_call_target="tpu_custom_call" | custom-call | flops 27394048 | bytes 6848512 | tf_op jit(solution)/shard_map/pallas_call | solution.py:140
  22.1 0.0 collective-permute-done.6.near_rows
  22.1 1.4 %collective-permute-done.7.far_rows = f32[46,8,128]{2,1,0:T(8,128)S(1)} collective-permute-done((f32[46,8,128]{2,1,0:T(8,128)S(1)}, f32[46,8,128]{2,1,0:T(8,128)S(1)}, u32[]{:S(2)}, u32[]{:S(2)}) %collective-permute-start.7) | collective-permute-done | bytes 188448 | tf_op jit(solution)/shard_map/ppermute | solution.py:654
  23.5 0.2 shard_map.61
  23.7 3.1 %shard_map.62 = (f32[4,64,128]{2,1,0:T(8,128)S(1)}, f32[4,64,128]{2,1,0:T(8,128)S(1)}, f32[12,24,128]{2,1,0:T(8,128)S(1)}) custom-call(f32[72,24,128]{2,1,0:T(8,128)S(1)} %get-tuple-element.48.wx, f32[72,24,128]{2,1,0:T(8,128)S(1)} %get-tuple-element.49.wy, f32[72,24,128]{2,1,0:T(8,128)S(1)} %get-tuple-element.50.wyp, ...), custom_call_target="tpu_custom_call" | custom-call | flops 32309248 | bytes 8077312 | tf_op jit(solution)/shard_map/pallas_call | solution.py:140
  26.8 0.6 %collective-permute-start.9 = (f32[4,64,128]{2,1,0:T(8,128)S(1)}, f32[4,64,128]{2,1,0:T(8,128)S(1)}, u32[]{:S(2)}, u32[]{:S(2)}) collective-permute-start(f32[4,64,128]{2,1,0:T(8,128)S(1)} %get-tuple-element.63), channel_id=1, source_target_pairs={{0,16},{16,0},{1,17},{17,1},{2,18},{18,2},{3,19},{19,3},{4,20},{20... | collective-permute-start | bytes 393224 | tf_op jit(solution)/shard_map/ppermute | solution.py:675
  27.4 0.0 collective-permute-done.8.refs_0_
  27.4 2.4 %shard_map.64 = (f32[4,64,128]{2,1,0:T(8,128)S(1)}, f32[4,64,128]{2,1,0:T(8,128)S(1)}) custom-call(f32[72,24,128]{2,1,0:T(8,128)S(1)} %get-tuple-element.48.wx, f32[72,24,128]{2,1,0:T(8,128)S(1)} %get-tuple-element.49.wy, f32[72,24,128]{2,1,0:T(8,128)S(1)} %get-tuple-element.50.wyp, f32[72,24,128]{2,1,0:T(8,128)S(1)} %get-tuple-element.51.wl, ...), custom_call_target="tpu_custom_call" | custom-call | flops 32505856 | bytes 8126464 | tf_op jit(solution)/shard_map/pallas_call | solution.py:140
  29.8 1.6 %collective-permute-start.10 = (f32[4,64,128]{2,1,0:T(8,128)S(1)}, f32[4,64,128]{2,1,0:T(8,128)S(1)}, u32[]{:S(2)}, u32[]{:S(2)}) collective-permute-start(f32[4,64,128]{2,1,0:T(8,128)S(1)} %get-tuple-element.64), channel_id=1, source_target_pairs={{0,16},{16,0},{1,17},{17,1},{2,18},{18,2},{3,19},{19,3},{4,20},{20... | collective-permute-start | bytes 393224 | tf_op jit(solution)/shard_map/ppermute | solution.py:679
  31.3 0.6 %collective-permute-done.9.got_low = f32[4,64,128]{2,1,0:T(8,128)S(1)} collective-permute-done((f32[4,64,128]{2,1,0:T(8,128)S(1)}, f32[4,64,128]{2,1,0:T(8,128)S(1)}, u32[]{:S(2)}, u32[]{:S(2)}) %collective-permute-start.9) | collective-permute-done | bytes 131104 | tf_op jit(solution)/shard_map/ppermute | solution.py:675
  31.9 0.5 %shard_map.65.most = f32[16,64,128]{2,1,0:T(8,128)S(1)} custom-call(f32[1024,128]{1,0:T(8,128)S(1)} %get-tuple-element.35.it, f32[4,64,128]{2,1,0:T(8,128)S(1)} %get-tuple-element.59.own_low, f32[4,64,128]{2,1,0:T(8,128)S(1)} %get-tuple-element.62.own_high, f32[4,64,128]{2,1,0:T(8,128)S(1)} %collective-permute-done.9.got_low), custom_call_target="tpu_custom_call" | custom-call | flops 5767168 | bytes 1441792 | tf_op jit(solution)/shard_map/pallas_call | solution.py:140
  32.5 2.3 %collective-permute-done.10.got_high = f32[4,64,128]{2,1,0:T(8,128)S(1)} collective-permute-done((f32[4,64,128]{2,1,0:T(8,128)S(1)}, f32[4,64,128]{2,1,0:T(8,128)S(1)}, u32[]{:S(2)}, u32[]{:S(2)}) %collective-permute-start.10) | collective-permute-done | bytes 131104 | tf_op jit(solution)/shard_map/ppermute | solution.py:679
  34.8 1.1 %shard_map.66 = f32[1024,128]{1,0:T(8,128)} custom-call(f32[16,64,128]{2,1,0:T(8,128)S(1)} %shard_map.65.most, f32[4,64,128]{2,1,0:T(8,128)S(1)} %collective-permute-done.10.got_high), custom_call_target="tpu_custom_call" | custom-call | flops 4718592 | bytes 1179648 | tf_op jit(solution)/shard_map/pallas_call | solution.py:140
  (6 shorter events, 0.0 us)
Async XLA Ops:
  0.0 3.5 %copy-start = (s32[64,16,128]{2,1,0:T(8,128)S(1)}, s32[64,16,128]{2,1,0:T(8,128)}, u32[]{:S(2)}) copy-start(s32[64,16,128]{2,1,0:T(8,128)} %param.8) | copy-start | bytes 1572868
  0.0 3.5 %copy-start.1 = (f32[64,16,128]{2,1,0:T(8,128)S(1)}, f32[64,16,128]{2,1,0:T(8,128)}, u32[]{:S(2)}) copy-start(f32[64,16,128]{2,1,0:T(8,128)} %param.7) | copy-start | bytes 1572868
  1.9 10.7 %collective-permute-start.4 = (f32[68,8,128]{2,1,0:T(8,128)S(1)}, f32[68,8,128]{2,1,0:T(8,128)S(1)}, u32[]{:S(2)}, u32[]{:S(2)}) collective-permute-start(f32[68,8,128]{2,1,0:T(8,128)S(1)} %get-tuple-element.43), channel_id=1, source_target_pairs={{0,16},{16,0},{1,17},{17,1},{2,18},{18,2},{3,19},{19,3},{4,20},{20... | collective-permute-start | bytes 835592 | tf_op jit(solution)/shard_map/ppermute | solution.py:628
  5.0 2.3 %collective-permute-start = (f32[6,16,128]{2,1,0:T(8,128)S(1)}, f32[6,16,128]{2,1,0:T(8,128)S(1)}, u32[]{:S(2)}, u32[]{:S(2)}) collective-permute-start(f32[6,16,128]{2,1,0:T(8,128)S(1)} %get-tuple-element.38), channel_id=1, source_target_pairs={{0,4},{8,12},{4,0},{12,8},{1,5},{9,13},{5,1},{13,9},{2,6},{10,14},... | collective-permute-start | bytes 147464 | tf_op jit(solution)/shard_map/ppermute | solution.py:638
  5.1 3.6 %collective-permute-start.1 = (f32[6,16,128]{2,1,0:T(8,128)S(1)}, f32[6,16,128]{2,1,0:T(8,128)S(1)}, u32[]{:S(2)}, u32[]{:S(2)}) collective-permute-start(f32[6,16,128]{2,1,0:T(8,128)S(1)} %get-tuple-element.39), channel_id=1, source_target_pairs={{4,8},{12,0},{8,4},{0,12},{5,9},{13,1},{9,5},{1,13},{6,10},{14,2},... | collective-permute-start | bytes 147464 | tf_op jit(solution)/shard_map/ppermute | solution.py:639
  6.7 10.1 %collective-permute-start.5 = (f32[68,8,128]{2,1,0:T(8,128)S(1)}, f32[68,8,128]{2,1,0:T(8,128)S(1)}, u32[]{:S(2)}, u32[]{:S(2)}) collective-permute-start(f32[68,8,128]{2,1,0:T(8,128)S(1)} %get-tuple-element.46), channel_id=1, source_target_pairs={{0,16},{16,0},{1,17},{17,1},{2,18},{18,2},{3,19},{19,3},{4,20},{20... | collective-permute-start | bytes 835592 | tf_op jit(solution)/shard_map/ppermute | solution.py:629
  9.0 8.4 %collective-permute-start.2 = (f32[44,8,128]{2,1,0:T(8,128)S(1)}, f32[44,8,128]{2,1,0:T(8,128)S(1)}, u32[]{:S(2)}, u32[]{:S(2)}) collective-permute-start(f32[44,8,128]{2,1,0:T(8,128)S(1)} %get-tuple-element.41), channel_id=1, source_target_pairs={{0,1},{2,3},{1,0},{3,2},{4,5},{6,7},{5,4},{7,6},{8,9},{10,11},{9,8... | collective-permute-start | bytes 540680 | tf_op jit(solution)/shard_map/ppermute | solution.py:647
  10.7 9.2 %collective-permute-start.3 = (f32[44,8,128]{2,1,0:T(8,128)S(1)}, f32[44,8,128]{2,1,0:T(8,128)S(1)}, u32[]{:S(2)}, u32[]{:S(2)}) collective-permute-start(f32[44,8,128]{2,1,0:T(8,128)S(1)} %get-tuple-element.42), channel_id=1, source_target_pairs={{1,2},{2,1},{5,6},{6,5},{9,10},{10,9},{13,14},{14,13},{17,18},{18,... | collective-permute-start | bytes 540680 | tf_op jit(solution)/shard_map/ppermute | solution.py:648
  12.8 9.3 %collective-permute-start.6 = (f32[46,8,128]{2,1,0:T(8,128)S(1)}, f32[46,8,128]{2,1,0:T(8,128)S(1)}, u32[]{:S(2)}, u32[]{:S(2)}) collective-permute-start(f32[46,8,128]{2,1,0:T(8,128)S(1)} %get-tuple-element.54), channel_id=1, source_target_pairs={{0,1},{2,3},{1,0},{3,2},{4,5},{6,7},{5,4},{7,6},{8,9},{10,11},{9,8... | collective-permute-start | bytes 565256 | tf_op jit(solution)/shard_map/ppermute | solution.py:653
  13.2 10.3 %collective-permute-start.7 = (f32[46,8,128]{2,1,0:T(8,128)S(1)}, f32[46,8,128]{2,1,0:T(8,128)S(1)}, u32[]{:S(2)}, u32[]{:S(2)}) collective-permute-start(f32[46,8,128]{2,1,0:T(8,128)S(1)} %get-tuple-element.55), channel_id=1, source_target_pairs={{1,2},{2,1},{5,6},{6,5},{9,10},{10,9},{13,14},{14,13},{17,18},{18,... | collective-permute-start | bytes 565256 | tf_op jit(solution)/shard_map/ppermute | solution.py:654
  19.9 7.4 %collective-permute-start.8 = (f32[4,24,128]{2,1,0:T(8,128)S(1)}, f32[4,24,128]{2,1,0:T(8,128)S(1)}, u32[]{:S(2)}, u32[]{:S(2)}) collective-permute-start(f32[4,24,128]{2,1,0:T(8,128)S(1)} %shard_map.63), channel_id=1, source_target_pairs={{0,16},{16,0},{1,17},{17,1},{2,18},{18,2},{3,19},{19,3},{4,20},{20... | collective-permute-start | bytes 147464 | tf_op jit(solution)/shard_map/ppermute | solution.py:657
  26.8 5.2 %collective-permute-start.9 = (f32[4,64,128]{2,1,0:T(8,128)S(1)}, f32[4,64,128]{2,1,0:T(8,128)S(1)}, u32[]{:S(2)}, u32[]{:S(2)}) collective-permute-start(f32[4,64,128]{2,1,0:T(8,128)S(1)} %get-tuple-element.63), channel_id=1, source_target_pairs={{0,16},{16,0},{1,17},{17,1},{2,18},{18,2},{3,19},{19,3},{4,20},{20... | collective-permute-start | bytes 393224 | tf_op jit(solution)/shard_map/ppermute | solution.py:675
  29.8 5.0 %collective-permute-start.10 = (f32[4,64,128]{2,1,0:T(8,128)S(1)}, f32[4,64,128]{2,1,0:T(8,128)S(1)}, u32[]{:S(2)}, u32[]{:S(2)}) collective-permute-start(f32[4,64,128]{2,1,0:T(8,128)S(1)} %get-tuple-element.64), channel_id=1, source_target_pairs={{0,16},{16,0},{1,17},{17,1},{2,18},{18,2},{3,19},{19,3},{4,20},{20... | collective-permute-start | bytes 393224 | tf_op jit(solution)/shard_map/ppermute | solution.py:679

commit v3 on v2

--- a/solution.py
+++ b/solution.py
@@ -212,7 +212,7 @@
     for k in range(ROWS // TILE):
         for copy in copies[4 * k : 4 * k + 4]:
             copy.wait()
-        blocks(k * TILE, (k + 1) * TILE, 4, turn)
+        blocks(k * TILE, (k + 1) * TILE, 8, turn)
     start = (LONS - SENT) * ROWS * (1 - t)
     top = ids(TILE, 0) < HALO
 
@@ -243,7 +243,7 @@
             value = jnp.where(classes == c, table[c], value)
         fixed[pl.ds(r, LONS, stride=ROWS), :] = cat(value, initial[rows, :]).T
 
-    blocks(0, ROWS, 4, turn)
+    blocks(0, ROWS, 8, turn)
     near_right = even("lon")
     low = in_low(ROWS)
 

time: 36.1 us -> 36 us (level)
  no operation moved by 1% of the time
where the time goes in v3:
time: 36 us; the launch traced here: 35.9 us
  starting transfers between devices  14.1 us (39%)
  Pallas kernels  13.4 us (37%)
  waiting for transfers between devices  8.22 us (23%)
    pallas_call x12, Pallas kernels, call(): pl.pallas_call(body, out_shape=outs, in_specs=specs(len(ins), hbm_ins), o...  13.4 us
    ppermute x1, starting transfers between devices, two_steps(): far_rows = lax.ppermute(far_rows, 'lat', pairs[1])  3.55 us
    ppermute x1, waiting for transfers between devices, two_steps(): far_lat = lax.ppermute(far_lat, 'lat', pairs[1])  2.46 us
    ppermute x1, waiting for transfers between devices, two_steps(): got_high = lax.ppermute(send_high, 'tm', swap)  2.32 us
    ppermute x1, starting transfers between devices, two_steps(): far_lat = lax.ppermute(far_lat, 'lat', pairs[1])  1.91 us
    ppermute x1, starting transfers between devices, two_steps(): near_lat = lax.ppermute(near_lat, 'lat', pairs[0])  1.64 us
    ppermute x1, starting transfers between devices, two_steps(): far_sides = lax.ppermute(far_sides, 'lon', round_lon[1])  1.64 us
    ppermute x1, starting transfers between devices, two_steps(): edges = lax.ppermute(edges, 'tm', swap)  1.56 us
  transfers between devices with their start and end apart: 11, of which 5 were waited for; matrix products, arithmetic and copies ran while one was open for 0% of the time, Pallas kernels for 29%

profile of v3, /device:TPU:16, one launch (start us, length us, event | category | flops | bytes accessed | tf_op | source)
XLA Modules:
  0.0 35.9 jit_solution(6605159153378467255)
XLA Ops:
  0.0 1.9 %shard_map.55 = (f32[68,8,128]{2,1,0:T(8,128)S(1)}, f32[68,8,128]{2,1,0:T(8,128)S(1)}, f32[2048,128]{1,0:T(8,128)S(1)}, f32[1024,128]{1,0:T(8,128)S(1)}) custom-call(f32[64,16,128]{2,1,0:T(8,128)} %bitcast.11, f32[64,16,128]{2,1,0:T(8,128)} %bitcast.12), custom_call_target="tpu_custom_call" | custom-call | flops 12713984 | bytes 3178496 | tf_op jit(solution)/shard_map/pallas_call | solution.py:140
  1.9 1.6 %collective-permute-start.4 = (f32[68,8,128]{2,1,0:T(8,128)S(1)}, f32[68,8,128]{2,1,0:T(8,128)S(1)}, u32[]{:S(2)}, u32[]{:S(2)}) collective-permute-start(f32[68,8,128]{2,1,0:T(8,128)S(1)} %get-tuple-element.43), channel_id=1, source_target_pairs={{0,16},{16,0},{1,17},{17,1},{2,18},{18,2},{3,19},{19,3},{4,20},{20... | collective-permute-start | bytes 835592 | tf_op jit(solution)/shard_map/ppermute | solution.py:628
  3.5 1.4 %shard_map.56 = (f32[2048,128]{1,0:T(8,128)S(1)}, f32[6,16,128]{2,1,0:T(8,128)S(1)}, f32[6,16,128]{2,1,0:T(8,128)S(1)}) custom-call(f32[2048,128]{1,0:T(8,128)S(1)} %get-tuple-element.36.turned, s32[1024,128]{1,0:T(8,128)S(1)} %bitcast.9, f32[1024,128]{1,0:T(8,128)S(1)} %bitcast.10, f32[8]{0:T(128)} %table_hbm.1), custom_call_target="tpu_custom_call" | custom-call | flops 12976256 | bytes 3244064 | tf_op jit(solution)/shard_map/pallas_call | solution.py:140
  4.9 0.1 collective-permute-start
  5.0 1.6 %collective-permute-start.1 = (f32[6,16,128]{2,1,0:T(8,128)S(1)}, f32[6,16,128]{2,1,0:T(8,128)S(1)}, u32[]{:S(2)}, u32[]{:S(2)}) collective-permute-start(f32[6,16,128]{2,1,0:T(8,128)S(1)} %get-tuple-element.39), channel_id=1, source_target_pairs={{4,8},{12,0},{8,4},{0,12},{5,9},{13,1},{9,5},{1,13},{6,10},{14,2},... | collective-permute-start | bytes 147464 | tf_op jit(solution)/shard_map/ppermute | solution.py:639
  6.6 0.5 %collective-permute-start.5 = (f32[68,8,128]{2,1,0:T(8,128)S(1)}, f32[68,8,128]{2,1,0:T(8,128)S(1)}, u32[]{:S(2)}, u32[]{:S(2)}) collective-permute-start(f32[68,8,128]{2,1,0:T(8,128)S(1)} %get-tuple-element.46), channel_id=1, source_target_pairs={{0,16},{16,0},{1,17},{17,1},{2,18},{18,2},{3,19},{19,3},{4,20},{20... | collective-permute-start | bytes 835592 | tf_op jit(solution)/shard_map/ppermute | solution.py:629
  7.2 0.0 collective-permute-done.near_sides
  7.2 1.4 %collective-permute-done.1.far_sides = f32[6,16,128]{2,1,0:T(8,128)S(1)} collective-permute-done((f32[6,16,128]{2,1,0:T(8,128)S(1)}, f32[6,16,128]{2,1,0:T(8,128)S(1)}, u32[]{:S(2)}, u32[]{:S(2)}) %collective-permute-start.1) | collective-permute-done | bytes 49184 | tf_op jit(solution)/shard_map/ppermute | solution.py:639
  8.6 0.4 %shard_map.57 = (f32[72,16,128]{2,1,0:T(8,128)S(1)}, f32[72,16,128]{2,1,0:T(8,128)S(1)}, f32[44,8,128]{2,1,0:T(8,128)S(1)}, f32[44,8,128]{2,1,0:T(8,128)S(1)}, f32[4,16,128]{2,1,0:T(8,128)S(1)}) custom-call(f32[128,16,128]{2,1,0:T(8,128)S(1)} %bitcast.7, f32[128,16,128]{2,1,0:T(8,128)S(1)} %bitcast.8, f32[6,16,128]{2,1,0:T(8,128)S(1)} %collective-permute-done.near_sides, ...), custom_call_target="tpu_custom_call" | custom-call | flops 15073280 | bytes 3768320 | tf_op jit(solution)/shard_map/pallas_call | solution.py:140
  9.0 1.6 %collective-permute-start.2 = (f32[44,8,128]{2,1,0:T(8,128)S(1)}, f32[44,8,128]{2,1,0:T(8,128)S(1)}, u32[]{:S(2)}, u32[]{:S(2)}) collective-permute-start(f32[44,8,128]{2,1,0:T(8,128)S(1)} %get-tuple-element.41), channel_id=1, source_target_pairs={{0,1},{2,3},{1,0},{3,2},{4,5},{6,7},{5,4},{7,6},{8,9},{10,11},{9,8... | collective-permute-start | bytes 540680 | tf_op jit(solution)/shard_map/ppermute | solution.py:647
  10.6 1.9 %collective-permute-start.3 = (f32[44,8,128]{2,1,0:T(8,128)S(1)}, f32[44,8,128]{2,1,0:T(8,128)S(1)}, u32[]{:S(2)}, u32[]{:S(2)}) collective-permute-start(f32[44,8,128]{2,1,0:T(8,128)S(1)} %get-tuple-element.42), channel_id=1, source_target_pairs={{1,2},{2,1},{5,6},{6,5},{9,10},{10,9},{13,14},{14,13},{17,18},{18,... | collective-permute-start | bytes 540680 | tf_op jit(solution)/shard_map/ppermute | solution.py:648
  12.5 0.0 collective-permute-done.4.edges
  12.5 0.2 shard_map.58
  12.8 0.4 %collective-permute-start.6 = (f32[46,8,128]{2,1,0:T(8,128)S(1)}, f32[46,8,128]{2,1,0:T(8,128)S(1)}, u32[]{:S(2)}, u32[]{:S(2)}) collective-permute-start(f32[46,8,128]{2,1,0:T(8,128)S(1)} %get-tuple-element.54), channel_id=1, source_target_pairs={{0,1},{2,3},{1,0},{3,2},{4,5},{6,7},{5,4},{7,6},{8,9},{10,11},{9,8... | collective-permute-start | bytes 565256 | tf_op jit(solution)/shard_map/ppermute | solution.py:653
  13.2 3.6 %collective-permute-start.7 = (f32[46,8,128]{2,1,0:T(8,128)S(1)}, f32[46,8,128]{2,1,0:T(8,128)S(1)}, u32[]{:S(2)}, u32[]{:S(2)}) collective-permute-start(f32[46,8,128]{2,1,0:T(8,128)S(1)} %get-tuple-element.55), channel_id=1, source_target_pairs={{1,2},{2,1},{5,6},{6,5},{9,10},{10,9},{13,14},{14,13},{17,18},{18,... | collective-permute-start | bytes 565256 | tf_op jit(solution)/shard_map/ppermute | solution.py:654
  16.8 0.0 collective-permute-done.5.middle
  16.8 0.6 %shard_map.59 = (f32[72,16,128]{2,1,0:T(8,128)S(1)}, f32[72,16,128]{2,1,0:T(8,128)S(1)}) custom-call(f32[68,8,128]{2,1,0:T(8,128)S(1)} %get-tuple-element.45.edges, f32[68,8,128]{2,1,0:T(8,128)S(1)} %collective-permute-done.5.middle, f32[72,16,128]{2,1,0:T(8,128)S(1)} %get-tuple-element.44.own, f32[72,16,128]{2,1,0:T(8,128)S(1)} %get-tuple-element.40.own_fixed), custom_call_target="tpu_custom_call" | custom-call | flops 11665408 | bytes 2916352 | tf_op jit(solution)/shard_map/pallas_call | solution.py:140
  17.4 2.5 %collective-permute-done.3.far_lat = f32[44,8,128]{2,1,0:T(8,128)S(1)} collective-permute-done((f32[44,8,128]{2,1,0:T(8,128)S(1)}, f32[44,8,128]{2,1,0:T(8,128)S(1)}, u32[]{:S(2)}, u32[]{:S(2)}) %collective-permute-start.3) | collective-permute-done | bytes 180256 | tf_op jit(solution)/shard_map/ppermute | solution.py:648
  19.9 0.6 %collective-permute-start.8 = (f32[4,24,128]{2,1,0:T(8,128)S(1)}, f32[4,24,128]{2,1,0:T(8,128)S(1)}, u32[]{:S(2)}, u32[]{:S(2)}) collective-permute-start(f32[4,24,128]{2,1,0:T(8,128)S(1)} %shard_map.63), channel_id=1, source_target_pairs={{0,16},{16,0},{1,17},{17,1},{2,18},{18,2},{3,19},{19,3},{4,20},{20... | collective-permute-start | bytes 147464 | tf_op jit(solution)/shard_map/ppermute | solution.py:657
  20.5 1.6 %shard_map.60 = (f32[72,24,128]{2,1,0:T(8,128)S(1)}, f32[72,24,128]{2,1,0:T(8,128)S(1)}, f32[72,24,128]{2,1,0:T(8,128)S(1)}, f32[72,24,128]{2,1,0:T(8,128)S(1)},...) custom-call(f32[72,16,128]{2,1,0:T(8,128)S(1)} %get-tuple-element.40.own_fixed, ...), custom_call_target="tpu_custom_call" | custom-call | flops 27394048 | bytes 6848512 | tf_op jit(solution)/shard_map/pallas_call | solution.py:140
  22.0 0.0 collective-permute-done.6.near_rows
  22.0 1.4 %collective-permute-done.7.far_rows = f32[46,8,128]{2,1,0:T(8,128)S(1)} collective-permute-done((f32[46,8,128]{2,1,0:T(8,128)S(1)}, f32[46,8,128]{2,1,0:T(8,128)S(1)}, u32[]{:S(2)}, u32[]{:S(2)}) %collective-permute-start.7) | collective-permute-done | bytes 188448 | tf_op jit(solution)/shard_map/ppermute | solution.py:654
  23.5 0.2 shard_map.61
  23.6 3.1 %shard_map.62 = (f32[4,64,128]{2,1,0:T(8,128)S(1)}, f32[4,64,128]{2,1,0:T(8,128)S(1)}, f32[12,24,128]{2,1,0:T(8,128)S(1)}) custom-call(f32[72,24,128]{2,1,0:T(8,128)S(1)} %get-tuple-element.48.wx, f32[72,24,128]{2,1,0:T(8,128)S(1)} %get-tuple-element.49.wy, f32[72,24,128]{2,1,0:T(8,128)S(1)} %get-tuple-element.50.wyp, ...), custom_call_target="tpu_custom_call" | custom-call | flops 32309248 | bytes 8077312 | tf_op jit(solution)/shard_map/pallas_call | solution.py:140
  26.7 0.6 %collective-permute-start.9 = (f32[4,64,128]{2,1,0:T(8,128)S(1)}, f32[4,64,128]{2,1,0:T(8,128)S(1)}, u32[]{:S(2)}, u32[]{:S(2)}) collective-permute-start(f32[4,64,128]{2,1,0:T(8,128)S(1)} %get-tuple-element.63), channel_id=1, source_target_pairs={{0,16},{16,0},{1,17},{17,1},{2,18},{18,2},{3,19},{19,3},{4,20},{20... | collective-permute-start | bytes 393224 | tf_op jit(solution)/shard_map/ppermute | solution.py:675
  27.3 0.0 collective-permute-done.8.refs_0_
  27.3 2.4 %shard_map.64 = (f32[4,64,128]{2,1,0:T(8,128)S(1)}, f32[4,64,128]{2,1,0:T(8,128)S(1)}) custom-call(f32[72,24,128]{2,1,0:T(8,128)S(1)} %get-tuple-element.48.wx, f32[72,24,128]{2,1,0:T(8,128)S(1)} %get-tuple-element.49.wy, f32[72,24,128]{2,1,0:T(8,128)S(1)} %get-tuple-element.50.wyp, f32[72,24,128]{2,1,0:T(8,128)S(1)} %get-tuple-element.51.wl, ...), custom_call_target="tpu_custom_call" | custom-call | flops 32505856 | bytes 8126464 | tf_op jit(solution)/shard_map/pallas_call | solution.py:140
  29.7 1.6 %collective-permute-start.10 = (f32[4,64,128]{2,1,0:T(8,128)S(1)}, f32[4,64,128]{2,1,0:T(8,128)S(1)}, u32[]{:S(2)}, u32[]{:S(2)}) collective-permute-start(f32[4,64,128]{2,1,0:T(8,128)S(1)} %get-tuple-element.64), channel_id=1, source_target_pairs={{0,16},{16,0},{1,17},{17,1},{2,18},{18,2},{3,19},{19,3},{4,20},{20... | collective-permute-start | bytes 393224 | tf_op jit(solution)/shard_map/ppermute | solution.py:679
  31.3 0.6 %collective-permute-done.9.got_low = f32[4,64,128]{2,1,0:T(8,128)S(1)} collective-permute-done((f32[4,64,128]{2,1,0:T(8,128)S(1)}, f32[4,64,128]{2,1,0:T(8,128)S(1)}, u32[]{:S(2)}, u32[]{:S(2)}) %collective-permute-start.9) | collective-permute-done | bytes 131104 | tf_op jit(solution)/shard_map/ppermute | solution.py:675
  31.9 0.5 %shard_map.65.most = f32[16,64,128]{2,1,0:T(8,128)S(1)} custom-call(f32[1024,128]{1,0:T(8,128)S(1)} %get-tuple-element.35.it, f32[4,64,128]{2,1,0:T(8,128)S(1)} %get-tuple-element.59.own_low, f32[4,64,128]{2,1,0:T(8,128)S(1)} %get-tuple-element.62.own_high, f32[4,64,128]{2,1,0:T(8,128)S(1)} %collective-permute-done.9.got_low), custom_call_target="tpu_custom_call" | custom-call | flops 5767168 | bytes 1441792 | tf_op jit(solution)/shard_map/pallas_call | solution.py:140
  32.4 2.3 %collective-permute-done.10.got_high = f32[4,64,128]{2,1,0:T(8,128)S(1)} collective-permute-done((f32[4,64,128]{2,1,0:T(8,128)S(1)}, f32[4,64,128]{2,1,0:T(8,128)S(1)}, u32[]{:S(2)}, u32[]{:S(2)}) %collective-permute-start.10) | collective-permute-done | bytes 131104 | tf_op jit(solution)/shard_map/ppermute | solution.py:679
  34.8 1.1 %shard_map.66 = f32[1024,128]{1,0:T(8,128)} custom-call(f32[16,64,128]{2,1,0:T(8,128)S(1)} %shard_map.65.most, f32[4,64,128]{2,1,0:T(8,128)S(1)} %collective-permute-done.10.got_high), custom_call_target="tpu_custom_call" | custom-call | flops 4718592 | bytes 1179648 | tf_op jit(solution)/shard_map/pallas_call | solution.py:140
  (6 shorter events, 0.0 us)
Async XLA Ops:
  0.0 3.5 %copy-start = (s32[64,16,128]{2,1,0:T(8,128)S(1)}, s32[64,16,128]{2,1,0:T(8,128)}, u32[]{:S(2)}) copy-start(s32[64,16,128]{2,1,0:T(8,128)} %param.8) | copy-start | bytes 1572868
  0.0 3.5 %copy-start.1 = (f32[64,16,128]{2,1,0:T(8,128)S(1)}, f32[64,16,128]{2,1,0:T(8,128)}, u32[]{:S(2)}) copy-start(f32[64,16,128]{2,1,0:T(8,128)} %param.7) | copy-start | bytes 1572868
  1.9 10.6 %collective-permute-start.4 = (f32[68,8,128]{2,1,0:T(8,128)S(1)}, f32[68,8,128]{2,1,0:T(8,128)S(1)}, u32[]{:S(2)}, u32[]{:S(2)}) collective-permute-start(f32[68,8,128]{2,1,0:T(8,128)S(1)} %get-tuple-element.43), channel_id=1, source_target_pairs={{0,16},{16,0},{1,17},{17,1},{2,18},{18,2},{3,19},{19,3},{4,20},{20... | collective-permute-start | bytes 835592 | tf_op jit(solution)/shard_map/ppermute | solution.py:628
  4.9 2.3 %collective-permute-start = (f32[6,16,128]{2,1,0:T(8,128)S(1)}, f32[6,16,128]{2,1,0:T(8,128)S(1)}, u32[]{:S(2)}, u32[]{:S(2)}) collective-permute-start(f32[6,16,128]{2,1,0:T(8,128)S(1)} %get-tuple-element.38), channel_id=1, source_target_pairs={{0,4},{8,12},{4,0},{12,8},{1,5},{9,13},{5,1},{13,9},{2,6},{10,14},... | collective-permute-start | bytes 147464 | tf_op jit(solution)/shard_map/ppermute | solution.py:638
  5.0 3.6 %collective-permute-start.1 = (f32[6,16,128]{2,1,0:T(8,128)S(1)}, f32[6,16,128]{2,1,0:T(8,128)S(1)}, u32[]{:S(2)}, u32[]{:S(2)}) collective-permute-start(f32[6,16,128]{2,1,0:T(8,128)S(1)} %get-tuple-element.39), channel_id=1, source_target_pairs={{4,8},{12,0},{8,4},{0,12},{5,9},{13,1},{9,5},{1,13},{6,10},{14,2},... | collective-permute-start | bytes 147464 | tf_op jit(solution)/shard_map/ppermute | solution.py:639
  6.6 10.1 %collective-permute-start.5 = (f32[68,8,128]{2,1,0:T(8,128)S(1)}, f32[68,8,128]{2,1,0:T(8,128)S(1)}, u32[]{:S(2)}, u32[]{:S(2)}) collective-permute-start(f32[68,8,128]{2,1,0:T(8,128)S(1)} %get-tuple-element.46), channel_id=1, source_target_pairs={{0,16},{16,0},{1,17},{17,1},{2,18},{18,2},{3,19},{19,3},{4,20},{20... | collective-permute-start | bytes 835592 | tf_op jit(solution)/shard_map/ppermute | solution.py:629
  9.0 8.4 %collective-permute-start.2 = (f32[44,8,128]{2,1,0:T(8,128)S(1)}, f32[44,8,128]{2,1,0:T(8,128)S(1)}, u32[]{:S(2)}, u32[]{:S(2)}) collective-permute-start(f32[44,8,128]{2,1,0:T(8,128)S(1)} %get-tuple-element.41), channel_id=1, source_target_pairs={{0,1},{2,3},{1,0},{3,2},{4,5},{6,7},{5,4},{7,6},{8,9},{10,11},{9,8... | collective-permute-start | bytes 540680 | tf_op jit(solution)/shard_map/ppermute | solution.py:647
  10.6 9.2 %collective-permute-start.3 = (f32[44,8,128]{2,1,0:T(8,128)S(1)}, f32[44,8,128]{2,1,0:T(8,128)S(1)}, u32[]{:S(2)}, u32[]{:S(2)}) collective-permute-start(f32[44,8,128]{2,1,0:T(8,128)S(1)} %get-tuple-element.42), channel_id=1, source_target_pairs={{1,2},{2,1},{5,6},{6,5},{9,10},{10,9},{13,14},{14,13},{17,18},{18,... | collective-permute-start | bytes 540680 | tf_op jit(solution)/shard_map/ppermute | solution.py:648
  12.8 9.3 %collective-permute-start.6 = (f32[46,8,128]{2,1,0:T(8,128)S(1)}, f32[46,8,128]{2,1,0:T(8,128)S(1)}, u32[]{:S(2)}, u32[]{:S(2)}) collective-permute-start(f32[46,8,128]{2,1,0:T(8,128)S(1)} %get-tuple-element.54), channel_id=1, source_target_pairs={{0,1},{2,3},{1,0},{3,2},{4,5},{6,7},{5,4},{7,6},{8,9},{10,11},{9,8... | collective-permute-start | bytes 565256 | tf_op jit(solution)/shard_map/ppermute | solution.py:653
  13.2 10.3 %collective-permute-start.7 = (f32[46,8,128]{2,1,0:T(8,128)S(1)}, f32[46,8,128]{2,1,0:T(8,128)S(1)}, u32[]{:S(2)}, u32[]{:S(2)}) collective-permute-start(f32[46,8,128]{2,1,0:T(8,128)S(1)} %get-tuple-element.55), channel_id=1, source_target_pairs={{1,2},{2,1},{5,6},{6,5},{9,10},{10,9},{13,14},{14,13},{17,18},{18,... | collective-permute-start | bytes 565256 | tf_op jit(solution)/shard_map/ppermute | solution.py:654
  19.9 7.4 %collective-permute-start.8 = (f32[4,24,128]{2,1,0:T(8,128)S(1)}, f32[4,24,128]{2,1,0:T(8,128)S(1)}, u32[]{:S(2)}, u32[]{:S(2)}) collective-permute-start(f32[4,24,128]{2,1,0:T(8,128)S(1)} %shard_map.63), channel_id=1, source_target_pairs={{0,16},{16,0},{1,17},{17,1},{2,18},{18,2},{3,19},{19,3},{4,20},{20... | collective-permute-start | bytes 147464 | tf_op jit(solution)/shard_map/ppermute | solution.py:657
  26.7 5.2 %collective-permute-start.9 = (f32[4,64,128]{2,1,0:T(8,128)S(1)}, f32[4,64,128]{2,1,0:T(8,128)S(1)}, u32[]{:S(2)}, u32[]{:S(2)}) collective-permute-start(f32[4,64,128]{2,1,0:T(8,128)S(1)} %get-tuple-element.63), channel_id=1, source_target_pairs={{0,16},{16,0},{1,17},{17,1},{2,18},{18,2},{3,19},{19,3},{4,20},{20... | collective-permute-start | bytes 393224 | tf_op jit(solution)/shard_map/ppermute | solution.py:675
  29.7 5.0 %collective-permute-start.10 = (f32[4,64,128]{2,1,0:T(8,128)S(1)}, f32[4,64,128]{2,1,0:T(8,128)S(1)}, u32[]{:S(2)}, u32[]{:S(2)}) collective-permute-start(f32[4,64,128]{2,1,0:T(8,128)S(1)} %get-tuple-element.64), channel_id=1, source_target_pairs={{0,16},{16,0},{1,17},{17,1},{2,18},{18,2},{3,19},{19,3},{4,20},{20... | collective-permute-start | bytes 393224 | tf_op jit(solution)/shard_map/ppermute | solution.py:679

commit v4 on v3

--- a/solution.py
+++ b/solution.py
@@ -299,7 +299,7 @@
         own[at] = heated(turned[lon], fixed[lon])
         own_fixed[at] = fixed[lon]
 
-    blocks(0, SENT, 17, copy)
+    blocks(0, SENT, 34, copy)
 
     def rows(i):
         near_lat[i], far_lat[i] = edge_pair(own[i], own[i + PAIRS])
@@ -597,7 +597,7 @@
                 out[pl.ds(c * part * ROWS + q + 4 * j, part, stride=ROWS), :] = jnp.where(here, old + placed(value, j, quarter), old)
         copy(c).start()
 
-    blocks(0, CHUNKS, 1, step)
+    blocks(0, CHUNKS, 2, step)
     for c in range(CHUNKS):
         copy(c).wait()
 

time: 36 us -> 35.9 us (level)
  no operation moved by 1% of the time
where the time goes in v4:
time: 35.9 us; the launch traced here: 35.7 us
  starting transfers between devices  14.1 us (39%)
  Pallas kernels  13.3 us (37%)
  waiting for transfers between devices  8.22 us (23%)
    pallas_call x12, Pallas kernels, call(): pl.pallas_call(body, out_shape=outs, in_specs=specs(len(ins), hbm_ins), o...  13.3 us
    ppermute x1, starting transfers between devices, two_steps(): far_rows = lax.ppermute(far_rows, 'lat', pairs[1])  3.54 us
    ppermute x1, waiting for transfers between devices, two_steps(): far_lat = lax.ppermute(far_lat, 'lat', pairs[1])  2.46 us
    ppermute x1, waiting for transfers between devices, two_steps(): got_high = lax.ppermute(send_high, 'tm', swap)  2.32 us
    ppermute x1, starting transfers between devices, two_steps(): far_lat = lax.ppermute(far_lat, 'lat', pairs[1])  1.91 us
    ppermute x1, starting transfers between devices, two_steps(): near_lat = lax.ppermute(near_lat, 'lat', pairs[0])  1.64 us
    ppermute x1, starting transfers between devices, two_steps(): far_sides = lax.ppermute(far_sides, 'lon', round_lon[1])  1.64 us
    ppermute x1, starting transfers between devices, two_steps(): edges = lax.ppermute(edges, 'tm', swap)  1.56 us
  transfers between devices with their start and end apart: 11, of which 5 were waited for; matrix products, arithmetic and copies ran while one was open for 0% of the time, Pallas kernels for 29%

profile of v4, /device:TPU:16, one launch (start us, length us, event | category | flops | bytes accessed | tf_op | source)
XLA Modules:
  0.0 35.7 jit_solution(5473943405466404054)
XLA Ops:
  0.0 1.9 %shard_map.55 = (f32[68,8,128]{2,1,0:T(8,128)S(1)}, f32[68,8,128]{2,1,0:T(8,128)S(1)}, f32[2048,128]{1,0:T(8,128)S(1)}, f32[1024,128]{1,0:T(8,128)S(1)}) custom-call(f32[64,16,128]{2,1,0:T(8,128)} %bitcast.11, f32[64,16,128]{2,1,0:T(8,128)} %bitcast.12), custom_call_target="tpu_custom_call" | custom-call | flops 12713984 | bytes 3178496 | tf_op jit(solution)/shard_map/pallas_call | solution.py:140
  1.9 1.6 %collective-permute-start.4 = (f32[68,8,128]{2,1,0:T(8,128)S(1)}, f32[68,8,128]{2,1,0:T(8,128)S(1)}, u32[]{:S(2)}, u32[]{:S(2)}) collective-permute-start(f32[68,8,128]{2,1,0:T(8,128)S(1)} %get-tuple-element.43), channel_id=1, source_target_pairs={{0,16},{16,0},{1,17},{17,1},{2,18},{18,2},{3,19},{19,3},{4,20},{20... | collective-permute-start | bytes 835592 | tf_op jit(solution)/shard_map/ppermute | solution.py:628
  3.5 1.4 %shard_map.56 = (f32[2048,128]{1,0:T(8,128)S(1)}, f32[6,16,128]{2,1,0:T(8,128)S(1)}, f32[6,16,128]{2,1,0:T(8,128)S(1)}) custom-call(f32[2048,128]{1,0:T(8,128)S(1)} %get-tuple-element.36.turned, s32[1024,128]{1,0:T(8,128)S(1)} %bitcast.9, f32[1024,128]{1,0:T(8,128)S(1)} %bitcast.10, f32[8]{0:T(128)} %table_hbm.1), custom_call_target="tpu_custom_call" | custom-call | flops 12976256 | bytes 3244064 | tf_op jit(solution)/shard_map/pallas_call | solution.py:140
  4.9 0.1 collective-permute-start
  5.0 1.6 %collective-permute-start.1 = (f32[6,16,128]{2,1,0:T(8,128)S(1)}, f32[6,16,128]{2,1,0:T(8,128)S(1)}, u32[]{:S(2)}, u32[]{:S(2)}) collective-permute-start(f32[6,16,128]{2,1,0:T(8,128)S(1)} %get-tuple-element.39), channel_id=1, source_target_pairs={{4,8},{12,0},{8,4},{0,12},{5,9},{13,1},{9,5},{1,13},{6,10},{14,2},... | collective-permute-start | bytes 147464 | tf_op jit(solution)/shard_map/ppermute | solution.py:639
  6.6 0.5 %collective-permute-start.5 = (f32[68,8,128]{2,1,0:T(8,128)S(1)}, f32[68,8,128]{2,1,0:T(8,128)S(1)}, u32[]{:S(2)}, u32[]{:S(2)}) collective-permute-start(f32[68,8,128]{2,1,0:T(8,128)S(1)} %get-tuple-element.46), channel_id=1, source_target_pairs={{0,16},{16,0},{1,17},{17,1},{2,18},{18,2},{3,19},{19,3},{4,20},{20... | collective-permute-start | bytes 835592 | tf_op jit(solution)/shard_map/ppermute | solution.py:629
  7.2 0.0 collective-permute-done.near_sides
  7.2 1.4 %collective-permute-done.1.far_sides = f32[6,16,128]{2,1,0:T(8,128)S(1)} collective-permute-done((f32[6,16,128]{2,1,0:T(8,128)S(1)}, f32[6,16,128]{2,1,0:T(8,128)S(1)}, u32[]{:S(2)}, u32[]{:S(2)}) %collective-permute-start.1) | collective-permute-done | bytes 49184 | tf_op jit(solution)/shard_map/ppermute | solution.py:639
  8.6 0.4 %shard_map.57 = (f32[72,16,128]{2,1,0:T(8,128)S(1)}, f32[72,16,128]{2,1,0:T(8,128)S(1)}, f32[44,8,128]{2,1,0:T(8,128)S(1)}, f32[44,8,128]{2,1,0:T(8,128)S(1)}, f32[4,16,128]{2,1,0:T(8,128)S(1)}) custom-call(f32[128,16,128]{2,1,0:T(8,128)S(1)} %bitcast.7, f32[128,16,128]{2,1,0:T(8,128)S(1)} %bitcast.8, f32[6,16,128]{2,1,0:T(8,128)S(1)} %collective-permute-done.near_sides, ...), custom_call_target="tpu_custom_call" | custom-call | flops 15073280 | bytes 3768320 | tf_op jit(solution)/shard_map/pallas_call | solution.py:140
  9.0 1.6 %collective-permute-start.2 = (f32[44,8,128]{2,1,0:T(8,128)S(1)}, f32[44,8,128]{2,1,0:T(8,128)S(1)}, u32[]{:S(2)}, u32[]{:S(2)}) collective-permute-start(f32[44,8,128]{2,1,0:T(8,128)S(1)} %get-tuple-element.41), channel_id=1, source_target_pairs={{0,1},{2,3},{1,0},{3,2},{4,5},{6,7},{5,4},{7,6},{8,9},{10,11},{9,8... | collective-permute-start | bytes 540680 | tf_op jit(solution)/shard_map/ppermute | solution.py:647
  10.6 1.9 %collective-permute-start.3 = (f32[44,8,128]{2,1,0:T(8,128)S(1)}, f32[44,8,128]{2,1,0:T(8,128)S(1)}, u32[]{:S(2)}, u32[]{:S(2)}) collective-permute-start(f32[44,8,128]{2,1,0:T(8,128)S(1)} %get-tuple-element.42), channel_id=1, source_target_pairs={{1,2},{2,1},{5,6},{6,5},{9,10},{10,9},{13,14},{14,13},{17,18},{18,... | collective-permute-start | bytes 540680 | tf_op jit(solution)/shard_map/ppermute | solution.py:648
  12.5 0.0 collective-permute-done.4.edges
  12.5 0.2 shard_map.58
  12.7 0.5 %collective-permute-start.6 = (f32[46,8,128]{2,1,0:T(8,128)S(1)}, f32[46,8,128]{2,1,0:T(8,128)S(1)}, u32[]{:S(2)}, u32[]{:S(2)}) collective-permute-start(f32[46,8,128]{2,1,0:T(8,128)S(1)} %get-tuple-element.54), channel_id=1, source_target_pairs={{0,1},{2,3},{1,0},{3,2},{4,5},{6,7},{5,4},{7,6},{8,9},{10,11},{9,8... | collective-permute-start | bytes 565256 | tf_op jit(solution)/shard_map/ppermute | solution.py:653
  13.2 3.5 %collective-permute-start.7 = (f32[46,8,128]{2,1,0:T(8,128)S(1)}, f32[46,8,128]{2,1,0:T(8,128)S(1)}, u32[]{:S(2)}, u32[]{:S(2)}) collective-permute-start(f32[46,8,128]{2,1,0:T(8,128)S(1)} %get-tuple-element.55), channel_id=1, source_target_pairs={{1,2},{2,1},{5,6},{6,5},{9,10},{10,9},{13,14},{14,13},{17,18},{18,... | collective-permute-start | bytes 565256 | tf_op jit(solution)/shard_map/ppermute | solution.py:654
  16.8 0.0 collective-permute-done.5.middle
  16.8 0.6 %shard_map.59 = (f32[72,16,128]{2,1,0:T(8,128)S(1)}, f32[72,16,128]{2,1,0:T(8,128)S(1)}) custom-call(f32[68,8,128]{2,1,0:T(8,128)S(1)} %get-tuple-element.45.edges, f32[68,8,128]{2,1,0:T(8,128)S(1)} %collective-permute-done.5.middle, f32[72,16,128]{2,1,0:T(8,128)S(1)} %get-tuple-element.44.own, f32[72,16,128]{2,1,0:T(8,128)S(1)} %get-tuple-element.40.own_fixed), custom_call_target="tpu_custom_call" | custom-call | flops 11665408 | bytes 2916352 | tf_op jit(solution)/shard_map/pallas_call | solution.py:140
  17.4 2.5 %collective-permute-done.3.far_lat = f32[44,8,128]{2,1,0:T(8,128)S(1)} collective-permute-done((f32[44,8,128]{2,1,0:T(8,128)S(1)}, f32[44,8,128]{2,1,0:T(8,128)S(1)}, u32[]{:S(2)}, u32[]{:S(2)}) %collective-permute-start.3) | collective-permute-done | bytes 180256 | tf_op jit(solution)/shard_map/ppermute | solution.py:648
  19.9 0.6 %collective-permute-start.8 = (f32[4,24,128]{2,1,0:T(8,128)S(1)}, f32[4,24,128]{2,1,0:T(8,128)S(1)}, u32[]{:S(2)}, u32[]{:S(2)}) collective-permute-start(f32[4,24,128]{2,1,0:T(8,128)S(1)} %shard_map.63), channel_id=1, source_target_pairs={{0,16},{16,0},{1,17},{17,1},{2,18},{18,2},{3,19},{19,3},{4,20},{20... | collective-permute-start | bytes 147464 | tf_op jit(solution)/shard_map/ppermute | solution.py:657
  20.5 1.6 %shard_map.60 = (f32[72,24,128]{2,1,0:T(8,128)S(1)}, f32[72,24,128]{2,1,0:T(8,128)S(1)}, f32[72,24,128]{2,1,0:T(8,128)S(1)}, f32[72,24,128]{2,1,0:T(8,128)S(1)},...) custom-call(f32[72,16,128]{2,1,0:T(8,128)S(1)} %get-tuple-element.40.own_fixed, ...), custom_call_target="tpu_custom_call" | custom-call | flops 27394048 | bytes 6848512 | tf_op jit(solution)/shard_map/pallas_call | solution.py:140
  22.0 0.0 collective-permute-done.6.near_rows
  22.0 1.4 %collective-permute-done.7.far_rows = f32[46,8,128]{2,1,0:T(8,128)S(1)} collective-permute-done((f32[46,8,128]{2,1,0:T(8,128)S(1)}, f32[46,8,128]{2,1,0:T(8,128)S(1)}, u32[]{:S(2)}, u32[]{:S(2)}) %collective-permute-start.7) | collective-permute-done | bytes 188448 | tf_op jit(solution)/shard_map/ppermute | solution.py:654
  23.4 0.2 shard_map.61
  23.6 3.1 %shard_map.62 = (f32[4,64,128]{2,1,0:T(8,128)S(1)}, f32[4,64,128]{2,1,0:T(8,128)S(1)}, f32[12,24,128]{2,1,0:T(8,128)S(1)}) custom-call(f32[72,24,128]{2,1,0:T(8,128)S(1)} %get-tuple-element.48.wx, f32[72,24,128]{2,1,0:T(8,128)S(1)} %get-tuple-element.49.wy, f32[72,24,128]{2,1,0:T(8,128)S(1)} %get-tuple-element.50.wyp, ...), custom_call_target="tpu_custom_call" | custom-call | flops 32309248 | bytes 8077312 | tf_op jit(solution)/shard_map/pallas_call | solution.py:140
  26.7 0.6 %collective-permute-start.9 = (f32[4,64,128]{2,1,0:T(8,128)S(1)}, f32[4,64,128]{2,1,0:T(8,128)S(1)}, u32[]{:S(2)}, u32[]{:S(2)}) collective-permute-start(f32[4,64,128]{2,1,0:T(8,128)S(1)} %get-tuple-element.63), channel_id=1, source_target_pairs={{0,16},{16,0},{1,17},{17,1},{2,18},{18,2},{3,19},{19,3},{4,20},{20... | collective-permute-start | bytes 393224 | tf_op jit(solution)/shard_map/ppermute | solution.py:675
  27.3 0.0 collective-permute-done.8.refs_0_
  27.3 2.4 %shard_map.64 = (f32[4,64,128]{2,1,0:T(8,128)S(1)}, f32[4,64,128]{2,1,0:T(8,128)S(1)}) custom-call(f32[72,24,128]{2,1,0:T(8,128)S(1)} %get-tuple-element.48.wx, f32[72,24,128]{2,1,0:T(8,128)S(1)} %get-tuple-element.49.wy, f32[72,24,128]{2,1,0:T(8,128)S(1)} %get-tuple-element.50.wyp, f32[72,24,128]{2,1,0:T(8,128)S(1)} %get-tuple-element.51.wl, ...), custom_call_target="tpu_custom_call" | custom-call | flops 32505856 | bytes 8126464 | tf_op jit(solution)/shard_map/pallas_call | solution.py:140
  29.7 1.6 %collective-permute-start.10 = (f32[4,64,128]{2,1,0:T(8,128)S(1)}, f32[4,64,128]{2,1,0:T(8,128)S(1)}, u32[]{:S(2)}, u32[]{:S(2)}) collective-permute-start(f32[4,64,128]{2,1,0:T(8,128)S(1)} %get-tuple-element.64), channel_id=1, source_target_pairs={{0,16},{16,0},{1,17},{17,1},{2,18},{18,2},{3,19},{19,3},{4,20},{20... | collective-permute-start | bytes 393224 | tf_op jit(solution)/shard_map/ppermute | solution.py:679
  31.3 0.6 %collective-permute-done.9.got_low = f32[4,64,128]{2,1,0:T(8,128)S(1)} collective-permute-done((f32[4,64,128]{2,1,0:T(8,128)S(1)}, f32[4,64,128]{2,1,0:T(8,128)S(1)}, u32[]{:S(2)}, u32[]{:S(2)}) %collective-permute-start.9) | collective-permute-done | bytes 131104 | tf_op jit(solution)/shard_map/ppermute | solution.py:675
  31.9 0.5 %shard_map.65.most = f32[16,64,128]{2,1,0:T(8,128)S(1)} custom-call(f32[1024,128]{1,0:T(8,128)S(1)} %get-tuple-element.35.it, f32[4,64,128]{2,1,0:T(8,128)S(1)} %get-tuple-element.59.own_low, f32[4,64,128]{2,1,0:T(8,128)S(1)} %get-tuple-element.62.own_high, f32[4,64,128]{2,1,0:T(8,128)S(1)} %collective-permute-done.9.got_low), custom_call_target="tpu_custom_call" | custom-call | flops 5767168 | bytes 1441792 | tf_op jit(solution)/shard_map/pallas_call | solution.py:140
  32.4 2.3 %collective-permute-done.10.got_high = f32[4,64,128]{2,1,0:T(8,128)S(1)} collective-permute-done((f32[4,64,128]{2,1,0:T(8,128)S(1)}, f32[4,64,128]{2,1,0:T(8,128)S(1)}, u32[]{:S(2)}, u32[]{:S(2)}) %collective-permute-start.10) | collective-permute-done | bytes 131104 | tf_op jit(solution)/shard_map/ppermute | solution.py:679
  34.7 1.0 %shard_map.66 = f32[1024,128]{1,0:T(8,128)} custom-call(f32[16,64,128]{2,1,0:T(8,128)S(1)} %shard_map.65.most, f32[4,64,128]{2,1,0:T(8,128)S(1)} %collective-permute-done.10.got_high), custom_call_target="tpu_custom_call" | custom-call | flops 4718592 | bytes 1179648 | tf_op jit(solution)/shard_map/pallas_call | solution.py:140
  (6 shorter events, 0.0 us)
Async XLA Ops:
  0.0 3.5 %copy-start = (s32[64,16,128]{2,1,0:T(8,128)S(1)}, s32[64,16,128]{2,1,0:T(8,128)}, u32[]{:S(2)}) copy-start(s32[64,16,128]{2,1,0:T(8,128)} %param.8) | copy-start | bytes 1572868
  0.0 3.5 %copy-start.1 = (f32[64,16,128]{2,1,0:T(8,128)S(1)}, f32[64,16,128]{2,1,0:T(8,128)}, u32[]{:S(2)}) copy-start(f32[64,16,128]{2,1,0:T(8,128)} %param.7) | copy-start | bytes 1572868
  1.9 10.6 %collective-permute-start.4 = (f32[68,8,128]{2,1,0:T(8,128)S(1)}, f32[68,8,128]{2,1,0:T(8,128)S(1)}, u32[]{:S(2)}, u32[]{:S(2)}) collective-permute-start(f32[68,8,128]{2,1,0:T(8,128)S(1)} %get-tuple-element.43), channel_id=1, source_target_pairs={{0,16},{16,0},{1,17},{17,1},{2,18},{18,2},{3,19},{19,3},{4,20},{20... | collective-permute-start | bytes 835592 | tf_op jit(solution)/shard_map/ppermute | solution.py:628
  4.9 2.3 %collective-permute-start = (f32[6,16,128]{2,1,0:T(8,128)S(1)}, f32[6,16,128]{2,1,0:T(8,128)S(1)}, u32[]{:S(2)}, u32[]{:S(2)}) collective-permute-start(f32[6,16,128]{2,1,0:T(8,128)S(1)} %get-tuple-element.38), channel_id=1, source_target_pairs={{0,4},{8,12},{4,0},{12,8},{1,5},{9,13},{5,1},{13,9},{2,6},{10,14},... | collective-permute-start | bytes 147464 | tf_op jit(solution)/shard_map/ppermute | solution.py:638
  5.0 3.6 %collective-permute-start.1 = (f32[6,16,128]{2,1,0:T(8,128)S(1)}, f32[6,16,128]{2,1,0:T(8,128)S(1)}, u32[]{:S(2)}, u32[]{:S(2)}) collective-permute-start(f32[6,16,128]{2,1,0:T(8,128)S(1)} %get-tuple-element.39), channel_id=1, source_target_pairs={{4,8},{12,0},{8,4},{0,12},{5,9},{13,1},{9,5},{1,13},{6,10},{14,2},... | collective-permute-start | bytes 147464 | tf_op jit(solution)/shard_map/ppermute | solution.py:639
  6.6 10.1 %collective-permute-start.5 = (f32[68,8,128]{2,1,0:T(8,128)S(1)}, f32[68,8,128]{2,1,0:T(8,128)S(1)}, u32[]{:S(2)}, u32[]{:S(2)}) collective-permute-start(f32[68,8,128]{2,1,0:T(8,128)S(1)} %get-tuple-element.46), channel_id=1, source_target_pairs={{0,16},{16,0},{1,17},{17,1},{2,18},{18,2},{3,19},{19,3},{4,20},{20... | collective-permute-start | bytes 835592 | tf_op jit(solution)/shard_map/ppermute | solution.py:629
  9.0 8.4 %collective-permute-start.2 = (f32[44,8,128]{2,1,0:T(8,128)S(1)}, f32[44,8,128]{2,1,0:T(8,128)S(1)}, u32[]{:S(2)}, u32[]{:S(2)}) collective-permute-start(f32[44,8,128]{2,1,0:T(8,128)S(1)} %get-tuple-element.41), channel_id=1, source_target_pairs={{0,1},{2,3},{1,0},{3,2},{4,5},{6,7},{5,4},{7,6},{8,9},{10,11},{9,8... | collective-permute-start | bytes 540680 | tf_op jit(solution)/shard_map/ppermute | solution.py:647
  10.6 9.2 %collective-permute-start.3 = (f32[44,8,128]{2,1,0:T(8,128)S(1)}, f32[44,8,128]{2,1,0:T(8,128)S(1)}, u32[]{:S(2)}, u32[]{:S(2)}) collective-permute-start(f32[44,8,128]{2,1,0:T(8,128)S(1)} %get-tuple-element.42), channel_id=1, source_target_pairs={{1,2},{2,1},{5,6},{6,5},{9,10},{10,9},{13,14},{14,13},{17,18},{18,... | collective-permute-start | bytes 540680 | tf_op jit(solution)/shard_map/ppermute | solution.py:648
  12.7 9.3 %collective-permute-start.6 = (f32[46,8,128]{2,1,0:T(8,128)S(1)}, f32[46,8,128]{2,1,0:T(8,128)S(1)}, u32[]{:S(2)}, u32[]{:S(2)}) collective-permute-start(f32[46,8,128]{2,1,0:T(8,128)S(1)} %get-tuple-element.54), channel_id=1, source_target_pairs={{0,1},{2,3},{1,0},{3,2},{4,5},{6,7},{5,4},{7,6},{8,9},{10,11},{9,8... | collective-permute-start | bytes 565256 | tf_op jit(solution)/shard_map/ppermute | solution.py:653
  13.2 10.2 %collective-permute-start.7 = (f32[46,8,128]{2,1,0:T(8,128)S(1)}, f32[46,8,128]{2,1,0:T(8,128)S(1)}, u32[]{:S(2)}, u32[]{:S(2)}) collective-permute-start(f32[46,8,128]{2,1,0:T(8,128)S(1)} %get-tuple-element.55), channel_id=1, source_target_pairs={{1,2},{2,1},{5,6},{6,5},{9,10},{10,9},{13,14},{14,13},{17,18},{18,... | collective-permute-start | bytes 565256 | tf_op jit(solution)/shard_map/ppermute | solution.py:654
  19.9 7.4 %collective-permute-start.8 = (f32[4,24,128]{2,1,0:T(8,128)S(1)}, f32[4,24,128]{2,1,0:T(8,128)S(1)}, u32[]{:S(2)}, u32[]{:S(2)}) collective-permute-start(f32[4,24,128]{2,1,0:T(8,128)S(1)} %shard_map.63), channel_id=1, source_target_pairs={{0,16},{16,0},{1,17},{17,1},{2,18},{18,2},{3,19},{19,3},{4,20},{20... | collective-permute-start | bytes 147464 | tf_op jit(solution)/shard_map/ppermute | solution.py:657
  26.7 5.2 %collective-permute-start.9 = (f32[4,64,128]{2,1,0:T(8,128)S(1)}, f32[4,64,128]{2,1,0:T(8,128)S(1)}, u32[]{:S(2)}, u32[]{:S(2)}) collective-permute-start(f32[4,64,128]{2,1,0:T(8,128)S(1)} %get-tuple-element.63), channel_id=1, source_target_pairs={{0,16},{16,0},{1,17},{17,1},{2,18},{18,2},{3,19},{19,3},{4,20},{20... | collective-permute-start | bytes 393224 | tf_op jit(solution)/shard_map/ppermute | solution.py:675
  29.7 5.0 %collective-permute-start.10 = (f32[4,64,128]{2,1,0:T(8,128)S(1)}, f32[4,64,128]{2,1,0:T(8,128)S(1)}, u32[]{:S(2)}, u32[]{:S(2)}) collective-permute-start(f32[4,64,128]{2,1,0:T(8,128)S(1)} %get-tuple-element.64), channel_id=1, source_target_pairs={{0,16},{16,0},{1,17},{17,1},{2,18},{18,2},{3,19},{19,3},{4,20},{20... | collective-permute-start | bytes 393224 | tf_op jit(solution)/shard_map/ppermute | solution.py:679

commit v5 on v3

--- a/solution.py
+++ b/solution.py
@@ -400,6 +400,10 @@
     return cat(*[ref[at, pl.ds(j, TILE, stride=3), :] for j in range(3)])
 
 
+def woven_at(row):
+    return row % 3 * TILE + row // 3
+
+
 def next_row(x):
     return cat(x[TILE:], pltpu.roll(x[:TILE], TILE - 1, 0))
 
@@ -546,13 +550,12 @@
         value = jnp.where(low, value + moved, moved - value) * back
         lon = at - base
         lon = jnp.where(first, HALF // 2 - 1 - lon, lon)
-        for j in range(3):
-            natural[pl.ds(lon * rows + j, TILE, stride=3), :] = value[j * TILE : (j + 1) * TILE]
+        natural[pl.ds(pl.multiple_of(lon * rows, TILE), rows), :] = value
 
     over(3, plain, z, last)
     count = HALF // 2
     for q in range(4):
-        turned = cat(*[natural[pl.ds(q + 4 * j, count, stride=rows), :] for j in range(4)]).T
+        turned = cat(*[natural[pl.ds(woven_at(q + 4 * j), count, stride=rows), :] for j in range(4)]).T
         step0, step1 = turned[:LEVELS], turned[LEVELS:]
         w_own[q] = jnp.where(first, step0, step1)
         w_send[q] = jnp.where(first, step1, step0)

time: 36 us -> 36 us (level)
  no operation moved by 1% of the time
where the time goes in v5:
time: 36 us; the launch traced here: 35.9 us
  starting transfers between devices  14.1 us (39%)
  Pallas kernels  13.4 us (37%)
  waiting for transfers between devices  8.22 us (23%)
    pallas_call x12, Pallas kernels, call(): pl.pallas_call(body, out_shape=outs, in_specs=specs(len(ins), hbm_ins), o...  13.4 us
    ppermute x1, starting transfers between devices, two_steps(): far_rows = lax.ppermute(far_rows, 'lat', pairs[1])  3.55 us
    ppermute x1, waiting for transfers between devices, two_steps(): far_lat = lax.ppermute(far_lat, 'lat', pairs[1])  2.46 us
    ppermute x1, waiting for transfers between devices, two_steps(): got_high = lax.ppermute(send_high, 'tm', swap)  2.32 us
    ppermute x1, starting transfers between devices, two_steps(): far_lat = lax.ppermute(far_lat, 'lat', pairs[1])  1.91 us
    ppermute x1, starting transfers between devices, two_steps(): near_lat = lax.ppermute(near_lat, 'lat', pairs[0])  1.64 us
    ppermute x1, starting transfers between devices, two_steps(): far_sides = lax.ppermute(far_sides, 'lon', round_lon[1])  1.64 us
    ppermute x1, starting transfers between devices, two_steps(): edges = lax.ppermute(edges, 'tm', swap)  1.56 us
  transfers between devices with their start and end apart: 11, of which 5 were waited for; matrix products, arithmetic and copies ran while one was open for 0% of the time, Pallas kernels for 29%

profile of v5, /device:TPU:16, one launch (start us, length us, event | category | flops | bytes accessed | tf_op | source)
XLA Modules:
  0.0 35.9 jit_solution(9682458725045837331)
XLA Ops:
  0.0 1.9 %shard_map.55 = (f32[68,8,128]{2,1,0:T(8,128)S(1)}, f32[68,8,128]{2,1,0:T(8,128)S(1)}, f32[2048,128]{1,0:T(8,128)S(1)}, f32[1024,128]{1,0:T(8,128)S(1)}) custom-call(f32[64,16,128]{2,1,0:T(8,128)} %bitcast.11, f32[64,16,128]{2,1,0:T(8,128)} %bitcast.12), custom_call_target="tpu_custom_call" | custom-call | flops 12713984 | bytes 3178496 | tf_op jit(solution)/shard_map/pallas_call | solution.py:140
  1.9 1.6 %collective-permute-start.4 = (f32[68,8,128]{2,1,0:T(8,128)S(1)}, f32[68,8,128]{2,1,0:T(8,128)S(1)}, u32[]{:S(2)}, u32[]{:S(2)}) collective-permute-start(f32[68,8,128]{2,1,0:T(8,128)S(1)} %get-tuple-element.43), channel_id=1, source_target_pairs={{0,16},{16,0},{1,17},{17,1},{2,18},{18,2},{3,19},{19,3},{4,20},{20... | collective-permute-start | bytes 835592 | tf_op jit(solution)/shard_map/ppermute | solution.py:631
  3.5 1.4 %shard_map.56 = (f32[2048,128]{1,0:T(8,128)S(1)}, f32[6,16,128]{2,1,0:T(8,128)S(1)}, f32[6,16,128]{2,1,0:T(8,128)S(1)}) custom-call(f32[2048,128]{1,0:T(8,128)S(1)} %get-tuple-element.36.turned, s32[1024,128]{1,0:T(8,128)S(1)} %bitcast.9, f32[1024,128]{1,0:T(8,128)S(1)} %bitcast.10, f32[8]{0:T(128)} %table_hbm.1), custom_call_target="tpu_custom_call" | custom-call | flops 12976256 | bytes 3244064 | tf_op jit(solution)/shard_map/pallas_call | solution.py:140
  4.9 0.1 collective-permute-start
  5.0 1.6 %collective-permute-start.1 = (f32[6,16,128]{2,1,0:T(8,128)S(1)}, f32[6,16,128]{2,1,0:T(8,128)S(1)}, u32[]{:S(2)}, u32[]{:S(2)}) collective-permute-start(f32[6,16,128]{2,1,0:T(8,128)S(1)} %get-tuple-element.39), channel_id=1, source_target_pairs={{4,8},{12,0},{8,4},{0,12},{5,9},{13,1},{9,5},{1,13},{6,10},{14,2},... | collective-permute-start | bytes 147464 | tf_op jit(solution)/shard_map/ppermute | solution.py:642
  6.6 0.5 %collective-permute-start.5 = (f32[68,8,128]{2,1,0:T(8,128)S(1)}, f32[68,8,128]{2,1,0:T(8,128)S(1)}, u32[]{:S(2)}, u32[]{:S(2)}) collective-permute-start(f32[68,8,128]{2,1,0:T(8,128)S(1)} %get-tuple-element.46), channel_id=1, source_target_pairs={{0,16},{16,0},{1,17},{17,1},{2,18},{18,2},{3,19},{19,3},{4,20},{20... | collective-permute-start | bytes 835592 | tf_op jit(solution)/shard_map/ppermute | solution.py:632
  7.2 0.0 collective-permute-done.near_sides
  7.2 1.4 %collective-permute-done.1.far_sides = f32[6,16,128]{2,1,0:T(8,128)S(1)} collective-permute-done((f32[6,16,128]{2,1,0:T(8,128)S(1)}, f32[6,16,128]{2,1,0:T(8,128)S(1)}, u32[]{:S(2)}, u32[]{:S(2)}) %collective-permute-start.1) | collective-permute-done | bytes 49184 | tf_op jit(solution)/shard_map/ppermute | solution.py:642
  8.6 0.4 %shard_map.57 = (f32[72,16,128]{2,1,0:T(8,128)S(1)}, f32[72,16,128]{2,1,0:T(8,128)S(1)}, f32[44,8,128]{2,1,0:T(8,128)S(1)}, f32[44,8,128]{2,1,0:T(8,128)S(1)}, f32[4,16,128]{2,1,0:T(8,128)S(1)}) custom-call(f32[128,16,128]{2,1,0:T(8,128)S(1)} %bitcast.7, f32[128,16,128]{2,1,0:T(8,128)S(1)} %bitcast.8, f32[6,16,128]{2,1,0:T(8,128)S(1)} %collective-permute-done.near_sides, ...), custom_call_target="tpu_custom_call" | custom-call | flops 15073280 | bytes 3768320 | tf_op jit(solution)/shard_map/pallas_call | solution.py:140
  9.0 1.6 %collective-permute-start.2 = (f32[44,8,128]{2,1,0:T(8,128)S(1)}, f32[44,8,128]{2,1,0:T(8,128)S(1)}, u32[]{:S(2)}, u32[]{:S(2)}) collective-permute-start(f32[44,8,128]{2,1,0:T(8,128)S(1)} %get-tuple-element.41), channel_id=1, source_target_pairs={{0,1},{2,3},{1,0},{3,2},{4,5},{6,7},{5,4},{7,6},{8,9},{10,11},{9,8... | collective-permute-start | bytes 540680 | tf_op jit(solution)/shard_map/ppermute | solution.py:650
  10.6 1.9 %collective-permute-start.3 = (f32[44,8,128]{2,1,0:T(8,128)S(1)}, f32[44,8,128]{2,1,0:T(8,128)S(1)}, u32[]{:S(2)}, u32[]{:S(2)}) collective-permute-start(f32[44,8,128]{2,1,0:T(8,128)S(1)} %get-tuple-element.42), channel_id=1, source_target_pairs={{1,2},{2,1},{5,6},{6,5},{9,10},{10,9},{13,14},{14,13},{17,18},{18,... | collective-permute-start | bytes 540680 | tf_op jit(solution)/shard_map/ppermute | solution.py:651
  12.5 0.0 collective-permute-done.4.edges
  12.5 0.2 shard_map.58
  12.8 0.4 %collective-permute-start.6 = (f32[46,8,128]{2,1,0:T(8,128)S(1)}, f32[46,8,128]{2,1,0:T(8,128)S(1)}, u32[]{:S(2)}, u32[]{:S(2)}) collective-permute-start(f32[46,8,128]{2,1,0:T(8,128)S(1)} %get-tuple-element.54), channel_id=1, source_target_pairs={{0,1},{2,3},{1,0},{3,2},{4,5},{6,7},{5,4},{7,6},{8,9},{10,11},{9,8... | collective-permute-start | bytes 565256 | tf_op jit(solution)/shard_map/ppermute | solution.py:656
  13.2 3.6 %collective-permute-start.7 = (f32[46,8,128]{2,1,0:T(8,128)S(1)}, f32[46,8,128]{2,1,0:T(8,128)S(1)}, u32[]{:S(2)}, u32[]{:S(2)}) collective-permute-start(f32[46,8,128]{2,1,0:T(8,128)S(1)} %get-tuple-element.55), channel_id=1, source_target_pairs={{1,2},{2,1},{5,6},{6,5},{9,10},{10,9},{13,14},{14,13},{17,18},{18,... | collective-permute-start | bytes 565256 | tf_op jit(solution)/shard_map/ppermute | solution.py:657
  16.8 0.0 collective-permute-done.5.middle
  16.8 0.6 %shard_map.59 = (f32[72,16,128]{2,1,0:T(8,128)S(1)}, f32[72,16,128]{2,1,0:T(8,128)S(1)}) custom-call(f32[68,8,128]{2,1,0:T(8,128)S(1)} %get-tuple-element.45.edges, f32[68,8,128]{2,1,0:T(8,128)S(1)} %collective-permute-done.5.middle, f32[72,16,128]{2,1,0:T(8,128)S(1)} %get-tuple-element.44.own, f32[72,16,128]{2,1,0:T(8,128)S(1)} %get-tuple-element.40.own_fixed), custom_call_target="tpu_custom_call" | custom-call | flops 11665408 | bytes 2916352 | tf_op jit(solution)/shard_map/pallas_call | solution.py:140
  17.4 2.5 %collective-permute-done.3.far_lat = f32[44,8,128]{2,1,0:T(8,128)S(1)} collective-permute-done((f32[44,8,128]{2,1,0:T(8,128)S(1)}, f32[44,8,128]{2,1,0:T(8,128)S(1)}, u32[]{:S(2)}, u32[]{:S(2)}) %collective-permute-start.3) | collective-permute-done | bytes 180256 | tf_op jit(solution)/shard_map/ppermute | solution.py:651
  19.9 0.6 %collective-permute-start.8 = (f32[4,24,128]{2,1,0:T(8,128)S(1)}, f32[4,24,128]{2,1,0:T(8,128)S(1)}, u32[]{:S(2)}, u32[]{:S(2)}) collective-permute-start(f32[4,24,128]{2,1,0:T(8,128)S(1)} %shard_map.63), channel_id=1, source_target_pairs={{0,16},{16,0},{1,17},{17,1},{2,18},{18,2},{3,19},{19,3},{4,20},{20... | collective-permute-start | bytes 147464 | tf_op jit(solution)/shard_map/ppermute | solution.py:660
  20.5 1.6 %shard_map.60 = (f32[72,24,128]{2,1,0:T(8,128)S(1)}, f32[72,24,128]{2,1,0:T(8,128)S(1)}, f32[72,24,128]{2,1,0:T(8,128)S(1)}, f32[72,24,128]{2,1,0:T(8,128)S(1)},...) custom-call(f32[72,16,128]{2,1,0:T(8,128)S(1)} %get-tuple-element.40.own_fixed, ...), custom_call_target="tpu_custom_call" | custom-call | flops 27394048 | bytes 6848512 | tf_op jit(solution)/shard_map/pallas_call | solution.py:140
  22.0 0.0 collective-permute-done.6.near_rows
  22.0 1.4 %collective-permute-done.7.far_rows = f32[46,8,128]{2,1,0:T(8,128)S(1)} collective-permute-done((f32[46,8,128]{2,1,0:T(8,128)S(1)}, f32[46,8,128]{2,1,0:T(8,128)S(1)}, u32[]{:S(2)}, u32[]{:S(2)}) %collective-permute-start.7) | collective-permute-done | bytes 188448 | tf_op jit(solution)/shard_map/ppermute | solution.py:657
  23.5 0.2 shard_map.61
  23.6 3.1 %shard_map.62 = (f32[4,64,128]{2,1,0:T(8,128)S(1)}, f32[4,64,128]{2,1,0:T(8,128)S(1)}, f32[12,24,128]{2,1,0:T(8,128)S(1)}) custom-call(f32[72,24,128]{2,1,0:T(8,128)S(1)} %get-tuple-element.48.wx, f32[72,24,128]{2,1,0:T(8,128)S(1)} %get-tuple-element.49.wy, f32[72,24,128]{2,1,0:T(8,128)S(1)} %get-tuple-element.50.wyp, ...), custom_call_target="tpu_custom_call" | custom-call | flops 32309248 | bytes 8077312 | tf_op jit(solution)/shard_map/pallas_call | solution.py:140
  26.7 0.6 %collective-permute-start.9 = (f32[4,64,128]{2,1,0:T(8,128)S(1)}, f32[4,64,128]{2,1,0:T(8,128)S(1)}, u32[]{:S(2)}, u32[]{:S(2)}) collective-permute-start(f32[4,64,128]{2,1,0:T(8,128)S(1)} %get-tuple-element.63), channel_id=1, source_target_pairs={{0,16},{16,0},{1,17},{17,1},{2,18},{18,2},{3,19},{19,3},{4,20},{20... | collective-permute-start | bytes 393224 | tf_op jit(solution)/shard_map/ppermute | solution.py:678
  27.3 0.0 collective-permute-done.8.refs_0_
  27.3 2.4 %shard_map.64 = (f32[4,64,128]{2,1,0:T(8,128)S(1)}, f32[4,64,128]{2,1,0:T(8,128)S(1)}) custom-call(f32[72,24,128]{2,1,0:T(8,128)S(1)} %get-tuple-element.48.wx, f32[72,24,128]{2,1,0:T(8,128)S(1)} %get-tuple-element.49.wy, f32[72,24,128]{2,1,0:T(8,128)S(1)} %get-tuple-element.50.wyp, f32[72,24,128]{2,1,0:T(8,128)S(1)} %get-tuple-element.51.wl, ...), custom_call_target="tpu_custom_call" | custom-call | flops 32505856 | bytes 8126464 | tf_op jit(solution)/shard_map/pallas_call | solution.py:140
  29.7 1.6 %collective-permute-start.10 = (f32[4,64,128]{2,1,0:T(8,128)S(1)}, f32[4,64,128]{2,1,0:T(8,128)S(1)}, u32[]{:S(2)}, u32[]{:S(2)}) collective-permute-start(f32[4,64,128]{2,1,0:T(8,128)S(1)} %get-tuple-element.64), channel_id=1, source_target_pairs={{0,16},{16,0},{1,17},{17,1},{2,18},{18,2},{3,19},{19,3},{4,20},{20... | collective-permute-start | bytes 393224 | tf_op jit(solution)/shard_map/ppermute | solution.py:682
  31.3 0.6 %collective-permute-done.9.got_low = f32[4,64,128]{2,1,0:T(8,128)S(1)} collective-permute-done((f32[4,64,128]{2,1,0:T(8,128)S(1)}, f32[4,64,128]{2,1,0:T(8,128)S(1)}, u32[]{:S(2)}, u32[]{:S(2)}) %collective-permute-start.9) | collective-permute-done | bytes 131104 | tf_op jit(solution)/shard_map/ppermute | solution.py:678
  31.9 0.5 %shard_map.65.most = f32[16,64,128]{2,1,0:T(8,128)S(1)} custom-call(f32[1024,128]{1,0:T(8,128)S(1)} %get-tuple-element.35.it, f32[4,64,128]{2,1,0:T(8,128)S(1)} %get-tuple-element.59.own_low, f32[4,64,128]{2,1,0:T(8,128)S(1)} %get-tuple-element.62.own_high, f32[4,64,128]{2,1,0:T(8,128)S(1)} %collective-permute-done.9.got_low), custom_call_target="tpu_custom_call" | custom-call | flops 5767168 | bytes 1441792 | tf_op jit(solution)/shard_map/pallas_call | solution.py:140
  32.4 2.3 %collective-permute-done.10.got_high = f32[4,64,128]{2,1,0:T(8,128)S(1)} collective-permute-done((f32[4,64,128]{2,1,0:T(8,128)S(1)}, f32[4,64,128]{2,1,0:T(8,128)S(1)}, u32[]{:S(2)}, u32[]{:S(2)}) %collective-permute-start.10) | collective-permute-done | bytes 131104 | tf_op jit(solution)/shard_map/ppermute | solution.py:682
  34.8 1.1 %shard_map.66 = f32[1024,128]{1,0:T(8,128)} custom-call(f32[16,64,128]{2,1,0:T(8,128)S(1)} %shard_map.65.most, f32[4,64,128]{2,1,0:T(8,128)S(1)} %collective-permute-done.10.got_high), custom_call_target="tpu_custom_call" | custom-call | flops 4718592 | bytes 1179648 | tf_op jit(solution)/shard_map/pallas_call | solution.py:140
  (6 shorter events, 0.0 us)
Async XLA Ops:
  0.0 3.5 %copy-start = (s32[64,16,128]{2,1,0:T(8,128)S(1)}, s32[64,16,128]{2,1,0:T(8,128)}, u32[]{:S(2)}) copy-start(s32[64,16,128]{2,1,0:T(8,128)} %param.8) | copy-start | bytes 1572868
  0.0 3.5 %copy-start.1 = (f32[64,16,128]{2,1,0:T(8,128)S(1)}, f32[64,16,128]{2,1,0:T(8,128)}, u32[]{:S(2)}) copy-start(f32[64,16,128]{2,1,0:T(8,128)} %param.7) | copy-start | bytes 1572868
  1.9 10.6 %collective-permute-start.4 = (f32[68,8,128]{2,1,0:T(8,128)S(1)}, f32[68,8,128]{2,1,0:T(8,128)S(1)}, u32[]{:S(2)}, u32[]{:S(2)}) collective-permute-start(f32[68,8,128]{2,1,0:T(8,128)S(1)} %get-tuple-element.43), channel_id=1, source_target_pairs={{0,16},{16,0},{1,17},{17,1},{2,18},{18,2},{3,19},{19,3},{4,20},{20... | collective-permute-start | bytes 835592 | tf_op jit(solution)/shard_map/ppermute | solution.py:631
  4.9 2.3 %collective-permute-start = (f32[6,16,128]{2,1,0:T(8,128)S(1)}, f32[6,16,128]{2,1,0:T(8,128)S(1)}, u32[]{:S(2)}, u32[]{:S(2)}) collective-permute-start(f32[6,16,128]{2,1,0:T(8,128)S(1)} %get-tuple-element.38), channel_id=1, source_target_pairs={{0,4},{8,12},{4,0},{12,8},{1,5},{9,13},{5,1},{13,9},{2,6},{10,14},... | collective-permute-start | bytes 147464 | tf_op jit(solution)/shard_map/ppermute | solution.py:641
  5.0 3.6 %collective-permute-start.1 = (f32[6,16,128]{2,1,0:T(8,128)S(1)}, f32[6,16,128]{2,1,0:T(8,128)S(1)}, u32[]{:S(2)}, u32[]{:S(2)}) collective-permute-start(f32[6,16,128]{2,1,0:T(8,128)S(1)} %get-tuple-element.39), channel_id=1, source_target_pairs={{4,8},{12,0},{8,4},{0,12},{5,9},{13,1},{9,5},{1,13},{6,10},{14,2},... | collective-permute-start | bytes 147464 | tf_op jit(solution)/shard_map/ppermute | solution.py:642
  6.6 10.1 %collective-permute-start.5 = (f32[68,8,128]{2,1,0:T(8,128)S(1)}, f32[68,8,128]{2,1,0:T(8,128)S(1)}, u32[]{:S(2)}, u32[]{:S(2)}) collective-permute-start(f32[68,8,128]{2,1,0:T(8,128)S(1)} %get-tuple-element.46), channel_id=1, source_target_pairs={{0,16},{16,0},{1,17},{17,1},{2,18},{18,2},{3,19},{19,3},{4,20},{20... | collective-permute-start | bytes 835592 | tf_op jit(solution)/shard_map/ppermute | solution.py:632
  9.0 8.4 %collective-permute-start.2 = (f32[44,8,128]{2,1,0:T(8,128)S(1)}, f32[44,8,128]{2,1,0:T(8,128)S(1)}, u32[]{:S(2)}, u32[]{:S(2)}) collective-permute-start(f32[44,8,128]{2,1,0:T(8,128)S(1)} %get-tuple-element.41), channel_id=1, source_target_pairs={{0,1},{2,3},{1,0},{3,2},{4,5},{6,7},{5,4},{7,6},{8,9},{10,11},{9,8... | collective-permute-start | bytes 540680 | tf_op jit(solution)/shard_map/ppermute | solution.py:650
  10.6 9.2 %collective-permute-start.3 = (f32[44,8,128]{2,1,0:T(8,128)S(1)}, f32[44,8,128]{2,1,0:T(8,128)S(1)}, u32[]{:S(2)}, u32[]{:S(2)}) collective-permute-start(f32[44,8,128]{2,1,0:T(8,128)S(1)} %get-tuple-element.42), channel_id=1, source_target_pairs={{1,2},{2,1},{5,6},{6,5},{9,10},{10,9},{13,14},{14,13},{17,18},{18,... | collective-permute-start | bytes 540680 | tf_op jit(solution)/shard_map/ppermute | solution.py:651
  12.8 9.3 %collective-permute-start.6 = (f32[46,8,128]{2,1,0:T(8,128)S(1)}, f32[46,8,128]{2,1,0:T(8,128)S(1)}, u32[]{:S(2)}, u32[]{:S(2)}) collective-permute-start(f32[46,8,128]{2,1,0:T(8,128)S(1)} %get-tuple-element.54), channel_id=1, source_target_pairs={{0,1},{2,3},{1,0},{3,2},{4,5},{6,7},{5,4},{7,6},{8,9},{10,11},{9,8... | collective-permute-start | bytes 565256 | tf_op jit(solution)/shard_map/ppermute | solution.py:656
  13.2 10.3 %collective-permute-start.7 = (f32[46,8,128]{2,1,0:T(8,128)S(1)}, f32[46,8,128]{2,1,0:T(8,128)S(1)}, u32[]{:S(2)}, u32[]{:S(2)}) collective-permute-start(f32[46,8,128]{2,1,0:T(8,128)S(1)} %get-tuple-element.55), channel_id=1, source_target_pairs={{1,2},{2,1},{5,6},{6,5},{9,10},{10,9},{13,14},{14,13},{17,18},{18,... | collective-permute-start | bytes 565256 | tf_op jit(solution)/shard_map/ppermute | solution.py:657
  19.9 7.4 %collective-permute-start.8 = (f32[4,24,128]{2,1,0:T(8,128)S(1)}, f32[4,24,128]{2,1,0:T(8,128)S(1)}, u32[]{:S(2)}, u32[]{:S(2)}) collective-permute-start(f32[4,24,128]{2,1,0:T(8,128)S(1)} %shard_map.63), channel_id=1, source_target_pairs={{0,16},{16,0},{1,17},{17,1},{2,18},{18,2},{3,19},{19,3},{4,20},{20... | collective-permute-start | bytes 147464 | tf_op jit(solution)/shard_map/ppermute | solution.py:660
  26.7 5.2 %collective-permute-start.9 = (f32[4,64,128]{2,1,0:T(8,128)S(1)}, f32[4,64,128]{2,1,0:T(8,128)S(1)}, u32[]{:S(2)}, u32[]{:S(2)}) collective-permute-start(f32[4,64,128]{2,1,0:T(8,128)S(1)} %get-tuple-element.63), channel_id=1, source_target_pairs={{0,16},{16,0},{1,17},{17,1},{2,18},{18,2},{3,19},{19,3},{4,20},{20... | collective-permute-start | bytes 393224 | tf_op jit(solution)/shard_map/ppermute | solution.py:678
  29.7 5.0 %collective-permute-start.10 = (f32[4,64,128]{2,1,0:T(8,128)S(1)}, f32[4,64,128]{2,1,0:T(8,128)S(1)}, u32[]{:S(2)}, u32[]{:S(2)}) collective-permute-start(f32[4,64,128]{2,1,0:T(8,128)S(1)} %get-tuple-element.64), channel_id=1, source_target_pairs={{0,16},{16,0},{1,17},{17,1},{2,18},{18,2},{3,19},{19,3},{4,20},{20... | collective-permute-start | bytes 393224 | tf_op jit(solution)/shard_map/ppermute | solution.py:682
